TPU v7x, 256 devices: a whole 4x4x8 slice. The times are simulated.
256 devices in a mesh: pipe: 8 (over z), tensor: 2 (over x_lo), dp: 16 (over y, x_hi, core).
Axes of the slice: x: 4 (x_hi: 2, x_lo: 2; x = x_hi * 2 + x_lo), y: 4, z: 8, core: 2. Of those that a mesh axis runs over, the one named last changes fastest.
Arguments:
- section_proj: bfloat16 [8, 4608, 2048], P('pipe', 'dp', 'tensor'), may hold values from -0.125 to 0.125
- attn_values: bfloat16 [8, 4, 512, 2048], P('pipe', None, 'dp', 'tensor'), may hold values from -6 to 6
- post_gain: float32 [8, 4608], P('pipe'), may hold values from 0.5 to 1.5
- section_input: bfloat16 [4, 512, 4608], P(None, 'dp'), may hold values from -6 to 6
- final_gain: float32 [4608], replicated, may hold values from 0.5 to 1.5
- embed_block: bfloat16 [2048, 4608], P('tensor'), may hold values from -0.26367188 to 0.26367188
- token_ids: int32 [4, 512], P(None, 'dp'), may hold values from 0 to 4095
- target_ids: int32 [4, 512], P(None, 'dp'), may hold values from 0 to 4095
- block_offset: int32 [1], replicated, may hold values from 0 to 2048
- rest_lse: float32 [4, 512], P(None, 'dp'), may hold values from 7 to 13
Outputs:
- proj_grad: float32 [8, 4608, 2048], P('pipe', 'dp', 'tensor')
- tied_grad: float32 [2048, 4608], P(('tensor', 'dp'), 'pipe')
Inputs may be any that keep to these rules, and one draw needn't show every extreme that they name: `token_ids`: token ids lie in [0, 4096); about half fall inside the block.
All inputs are finite; a program needn't handle non-finite values.
Results may differ from a plain program's by a relative error of at most 0.028.
Values may be sent and summed in bfloat16 or wider, within the bound.
A program may use at most 128 MiB of HBM per device.

v0:
```python
import math

import jax
import jax.numpy as jnp
from jax import lax
from jax.sharding import PartitionSpec as P

EPS = 1e-06
CAP = 30.0


def broadcast(block, axis, owner):
    block = jnp.where(lax.axis_index(axis) == owner, block, jnp.zeros_like(block))
    return lax.psum(block, axis)


def normalize(value):
    scale = lax.rsqrt(jnp.mean(value * value, axis=-1, keepdims=True) + EPS)
    return (scale, value * scale)


def norm_back(scale, normed, grad):
    return scale * (grad - normed * jnp.mean(grad * normed, axis=-1, keepdims=True))


def per_device(
    section_proj,
    attn_values,
    post_gain,
    section_input,
    final_gain,
    embed_block,
    token_ids,
    target_ids,
    block_offset,
    rest_lse,
):
    n_pipe = lax.axis_size("pipe")
    section = lax.axis_index("pipe")
    is_last = section == n_pipe - 1
    is_first = section == 0
    weight = section_proj[0]
    micro, tokens, width = (attn_values.shape[1], attn_values.shape[2], attn_values.shape[3])
    count = micro * tokens
    values = attn_values[0].reshape(count, width)
    gain = post_gain[0]
    model = section_input.shape[2]
    contract_last = (((1,), (1,)), ((), ()))
    contract_first = (((0,), (0,)), ((), ()))
    partial_out = lax.dot_general(
        values,
        lax.all_gather(weight, "dp", axis=0, tiled=True),
        contract_last,
        preferred_element_type=jnp.float32,
    )
    output = lax.psum(partial_out.astype(jnp.bfloat16), "tensor").astype(jnp.float32)
    out_scale, out_normed = normalize(output)
    resid = section_input.reshape(count, model).astype(jnp.float32) + out_normed * gain
    y_scale, y_normed = normalize(resid)
    head_in = (y_normed * final_gain).astype(jnp.bfloat16)
    raw = lax.dot_general(head_in, embed_block, contract_last, preferred_element_type=jnp.float32)
    capped = jnp.tanh(raw / CAP)
    logits = CAP * capped
    total = lax.psum(jnp.sum(jnp.exp(logits), axis=1), "tensor")
    lse = jnp.logaddexp(rest_lse.reshape(count), jnp.log(total))
    vrows = embed_block.shape[0]
    first_row = block_offset[0] + lax.axis_index("tensor") * vrows
    column = lax.broadcasted_iota(jnp.int32, (count, vrows), 1)
    hit = (target_ids.reshape(count, 1) - first_row == column).astype(jnp.float32)
    delta = ((jnp.exp(logits - lse[:, None]) - hit) * (1.0 - capped * capped)).astype(jnp.bfloat16)
    back = lax.psum(
        jnp.dot(delta, embed_block, preferred_element_type=jnp.float32).astype(jnp.bfloat16),
        "tensor",
    ).astype(jnp.float32)
    top_grad = norm_back(y_scale, y_normed, back * final_gain).astype(jnp.bfloat16)
    top_grad = jnp.where(is_last, top_grad, jnp.zeros_like(top_grad))
    section_grad = broadcast(top_grad, "pipe", n_pipe - 1)
    out_grad = norm_back(out_scale, out_normed, section_grad.astype(jnp.float32) * gain).astype(
        jnp.bfloat16
    )
    own_grad = lax.psum_scatter(
        lax.dot_general(
            out_grad, values, contract_first, preferred_element_type=jnp.float32
        ).astype(jnp.bfloat16),
        "dp",
        scatter_dimension=0,
        tiled=True,
    ).astype(jnp.float32)
    head_term = lax.dot_general(delta, head_in, contract_first, preferred_element_type=jnp.float32)
    used = (token_ids.reshape(count, 1) - first_row == column).astype(jnp.bfloat16)
    embed_term = math.sqrt(model) * lax.dot_general(
        used, section_grad, contract_first, preferred_element_type=jnp.float32
    )
    zeros_term = jnp.zeros_like(head_term)
    term = jnp.where(is_last, head_term, zeros_term) + jnp.where(is_first, embed_term, zeros_term)
    shared = lax.psum_scatter(term.astype(jnp.bfloat16), "dp", scatter_dimension=0, tiled=True)
    tied = lax.psum_scatter(shared, "pipe", scatter_dimension=1, tiled=True).astype(jnp.float32)
    return (own_grad[None], tied)


def solution(mesh):
    in_specs = (
        P("pipe", "dp", "tensor"),
        P("pipe", None, "dp", "tensor"),
        P("pipe", None),
        P(None, "dp", None),
        P(),
        P("tensor", None),
        P(None, "dp"),
        P(None, "dp"),
        P(),
        P(None, "dp"),
    )
    out_specs = (P("pipe", "dp", "tensor"), P(("tensor", "dp"), "pipe"))
    return jax.shard_map(
        per_device, mesh=mesh, in_specs=in_specs, out_specs=out_specs, check_vma=False
    )
```

profile of v0, /device:TPU:1, one launch (start us, length us, event | category | flops | bytes accessed | tf_op | source)
XLA Modules:
  0.0 613.5 jit_solution(745249914637506768)
XLA Ops:
  7.2 0.7 all-gather.3.cloned.1.call-update
  8.0 89.5 %all-gather.3.cloned.1.call-done = bf16[1,4608,1024]{2,1,0:T(8,128)(2,1)} async-done(((bf16[1,288,1024]{2,1,0:T(8,128)(2,1)}), bf16[1,4608,1024]{2,1,0:T(8,128)(2,1)}) %all-gather.3.cloned.1.call-update) | async-done | bytes 9437200 | tf_op jit(solution)/shard_map/all_gather | solution.py:52
  97.5 8.0 %fusion.2 = bf16[128,4608]{1,0:T(8,128)(2,1)} fusion(bf16[128,1024]{1,0:T(8,128)(2,1)S(1)} %bitcast.22, bf16[1,4608,1024]{2,1,0:T(8,128)(2,1)} %all-gather.3.cloned.1.call-done), kind=kOutput, calls=%fused_computation.4 | convolution fusion | flops 1208549376 | bytes 10878976 | tf_op jit(solution)/shard_map/dot_general | solution.py:50
  106.4 51.3 %all-reduce.4.cloned.1.call-done = bf16[128,4608]{1,0:T(8,128)(2,1)} async-done(((bf16[128,4608]{1,0:T(8,128)(2,1)}), bf16[128,4608]{1,0:T(8,128)(2,1)}) %all-reduce.4.cloned.1.call-update) | async-done | bytes 1179664 | tf_op jit(solution)/shard_map/psum | solution.py:56
  157.7 1.6 fusion.13
  159.3 2.3 multiply_reduce_fusion.1
  161.7 7.0 %exponential_reduce_fusion = (f32[128]{0:T(128)S(1)}, f32[128,1024]{1,0:T(8,128)S(1)}) fusion(bf16[1024,4608]{1,0:T(8,128)(2,1)} %param.15, f32[128,4608]{1,0:T(8,128)S(1)} %get-tuple-element.3, f32[4608]{0:T(1024)S(1)} %copy-done.4, f32[128]{0:T(128)S(1)} %add_rsqrt_fusion), kind=kOutput, calls=%fused_computation.34 | convolution fusion | flops 1210122112 | bytes 12340224 | tf_op jit(solution)/shard_map/dot_general | solution.py:61
  168.7 3.8 psum.29
  172.5 6.2 %convolution_convert_fusion.1 = bf16[128,4608]{1,0:T(8,128)(2,1)} fusion(bf16[1024,4608]{1,0:T(8,128)(2,1)} %param.15, f32[128,1024]{1,0:T(8,128)S(1)} %get-tuple-element.5, s32[128]{0:T(128)S(1)} %sub.57, f32[128]{0:T(128)S(1)} %compare_select_fusion), kind=kOutput, calls=%fused_computation.5 | convolution fusion | flops 1209729024 | bytes 11142144 | tf_op jit(solution)/shard_map/dot_general | solution.py:72
  178.8 56.9 %all-reduce.6.cloned.1.call-done = bf16[128,4608]{1,0:T(8,128)(2,1)} async-done(((bf16[128,4608]{1,0:T(8,128)(2,1)}), bf16[128,4608]{1,0:T(8,128)(2,1)}) %all-reduce.6.cloned.1.call-update) | async-done | bytes 1179664 | tf_op jit(solution)/shard_map/psum | solution.py:71
  235.7 1.9 multiply_reduce_fusion
  237.6 1.7 fusion.16
  239.5 73.6 %all-reduce.8.cloned.1.call-done = bf16[128,4608]{1,0:T(8,128)(2,1)} async-done(((bf16[128,4608]{1,0:T(8,128)(2,1)}), bf16[128,4608]{1,0:T(8,128)(2,1)}) %all-reduce.8.cloned.1.call-update) | async-done | bytes 1179664 | tf_op jit(solution)/shard_map/psum | solution.py:14
  313.1 9.2 %fusion.21 = f32[1024,4608]{1,0:T(8,128)} fusion(bf16[128,4608]{1,0:T(8,128)(2,1)} %all-reduce.8.cloned.1.call-done, s32[128]{0:T(128)S(1)} %sub.64), kind=kOutput, calls=%fused_computation.35 | convolution fusion | flops 1208090624 | bytes 20054528 | tf_op jit(solution)/shard_map/dot_general | solution.py:91
  322.4 10.5 %add_convert_fusion = bf16[1024,4608]{1,0:T(8,128)(2,1)} fusion(f32[1024,4608]{1,0:T(8,128)} %fusion.21, pred[]{:T(512)S(6)} %eq.26, pred[]{:T(512)S(6)} %eq.23, f32[128,4608]{1,0:T(8,128)S(1)} %get-tuple-element.3, f32[4608]{0:T(1024)S(1)} %copy-done.4, f32[128]{0:T(128)S(1)} %add_rsqrt_fusion, f32[128,1024]{1,0:T(8,128)S(1)} %get-tuple-element.5, ...), kind=kOutput, calls=%fused_computation | convolution fusion | flops 1234501632 | bytes 31215106 | tf_op jit(solution)/shard_map/dot_general | solution.py:89
  333.1 1.0 copy-done.1
  335.1 5.3 convolution_convert_fusion
  340.5 108.6 %reduce-scatter.8.cloned.1.call-done = bf16[64,4608]{1,0:T(8,128)(2,1)} async-done(((bf16[1024,4608]{1,0:T(8,128)(2,1)}), bf16[64,4608]{1,0:T(8,128)(2,1)}) %reduce-scatter.8.cloned.1.call-update) | async-done | bytes 589840 | tf_op jit(solution)/shard_map/reduce_scatter | solution.py:96
  449.1 2.3 copy.12
  451.4 116.4 %reduce-scatter.6.cloned.1.call-done = bf16[288,1024]{1,0:T(8,128)(2,1)} async-done(((bf16[4608,1024]{1,0:T(8,128)(2,1)}), bf16[288,1024]{1,0:T(8,128)(2,1)}) %reduce-scatter.6.cloned.1.call-update) | async-done | bytes 589840 | tf_op jit(solution)/shard_map/reduce_scatter | solution.py:81
  567.8 2.2 bitcast_convert_fusion
  570.0 35.0 %reduce-scatter.10.cloned.1.call-done = bf16[576,64]{1,0:T(8,128)(2,1)} async-done(((bf16[4608,64]{1,0:T(8,128)(2,1)}), bf16[576,64]{1,0:T(8,128)(2,1)}) %reduce-scatter.10.cloned.1.call-update) | async-done | bytes 73744
  605.0 1.0 copy.13
  606.0 0.7 convert_element_type.61
  (42 shorter events, 1.9 us)
Async XLA Ops:
  7.2 90.3 %copy-start = (bf16[1,4,32,1024]{3,2,1,0:T(8,128)(2,1)S(1)}, bf16[1,4,32,1024]{3,2,1,0:T(8,128)(2,1)}, u32[]{:S(2)}) copy-start(bf16[1,4,32,1024]{3,2,1,0:T(8,128)(2,1)} %param.11) | copy-start | bytes 786436
  7.2 90.3 %all-gather.3.cloned.1.call-start = ((), (), s32[]{:S(2)}) async-start(), calls=%async_computation.8 | async-start | bytes 10027008 | tf_op jit(solution)/shard_map/all_gather | solution.py:52
  7.9 149.8 %all-reduce.4.cloned.1.call-start = ((), (), s32[]{:S(2)}) async-start(), calls=%async_computation.3 | async-start | bytes 2359296 | tf_op jit(solution)/shard_map/psum | solution.py:56
  97.5 8.7 %copy-start.6 = (f32[4,32]{1,0:T(4,128)S(1)}, f32[4,32]{1,0:T(4,128)}, u32[]{:S(2)}) copy-start(f32[4,32]{1,0:T(4,128)} %param.19) | copy-start | bytes 1540
  97.5 8.8 %copy-start.7 = (s32[4,32]{1,0:T(4,128)S(1)}, s32[4,32]{1,0:T(4,128)}, u32[]{:S(2)}) copy-start(s32[4,32]{1,0:T(4,128)} %param.17) | copy-start | bytes 1540
  97.5 8.9 %copy-start.5 = (f32[1,4608]{1,0:T(1,128)S(1)}, f32[1,4608]{1,0:T(1,128)}, u32[]{:S(2)}) copy-start(f32[1,4608]{1,0:T(1,128)} %param.12) | copy-start | bytes 55300
  105.5 130.2 %all-reduce.6.cloned.1.call-start = ((), (), s32[]{:S(2)}) async-start(), calls=%async_computation.4 | async-start | bytes 2359296 | tf_op jit(solution)/shard_map/psum | solution.py:71
  159.3 2.3 copy-start.4
  178.7 134.4 %all-reduce.8.cloned.1.call-start = ((), (), s32[]{:S(2)}) async-start(), calls=%async_computation.5 | async-start | bytes 2359296 | tf_op jit(solution)/shard_map/psum | solution.py:14
  235.7 1.9 copy-start.3
  237.6 1.8 copy-start.8
  239.3 209.8 %reduce-scatter.8.cloned.1.call-start = ((), (), s32[]{:S(2)}) async-start(), calls=%async_computation.7 | async-start | bytes 10027008 | tf_op jit(solution)/shard_map/reduce_scatter | solution.py:96
  332.9 1.3 copy-start.1
  332.9 1.6 copy-start.2
  332.9 234.8 %reduce-scatter.6.cloned.1.call-start = ((), (), s32[]{:S(2)}) async-start(), calls=%async_computation.6 | async-start | bytes 10027008 | tf_op jit(solution)/shard_map/reduce_scatter | solution.py:81
  340.5 264.5 %reduce-scatter.10.cloned.1.call-start = ((), (), s32[]{:S(2)}) async-start(), calls=%async_computation.9 | async-start | bytes 1327104
Sparse Core Ops, SparseCore 0:
  10.8 86.6 all-gather.2
  105.6 52.0 all-reduce.3
  178.9 56.7 all-reduce.5
  239.5 73.6 all-reduce.7
  333.0 116.0 reduce-scatter.7
  454.3 113.4 reduce-scatter.5
  570.3 34.6 reduce-scatter.9
where the time goes:
time: 617 us; the launch traced here: 614 us
  waiting for transfers between devices  532 us (86%)
  matrix products  46.3 us (8%)
  between operations  14.9 us (2%)
  other arithmetic  11.1 us (2%)
    reduce_scatter x1, waiting for transfers between devices, per_device(): lax.psum_scatter(lax.dot_general(out_grad, values, contract_first, prefer...  116 us
    reduce_scatter x1, waiting for transfers between devices, per_device(): lax.psum_scatter(term.astype(jnp.bfloat16), 'dp', scatter_dimension=0, ti...  109 us
    all_gather x1, waiting for transfers between devices, per_device(): lax.all_gather(weight, 'dp', axis=0, tiled=True)  89.5 us
    psum x1, waiting for transfers between devices, broadcast(): return lax.psum(block, axis)  73.6 us
    psum x1, waiting for transfers between devices, per_device(): lax.psum(jnp.dot(delta, embed_block, preferred_element_type=jnp.float32)....  56.9 us
    psum x1, waiting for transfers between devices, per_device(): lax.psum(partial_out.astype(jnp.bfloat16), 'tensor').astype(jnp.float32)  51.3 us
    unnamed x8, waiting for transfers between devices  35.8 us
  transfers between devices with their start and end apart: 7, of which 7 were waited for; matrix products, arithmetic and copies ran while one was open for 2% of the time, Pallas kernels for 0%

commit v1 on v0

v1 whole, which is shorter than its diff:
```python
import functools
import math

import jax
import jax.numpy as jnp
from jax import lax
from jax.experimental import pallas as pl
from jax.experimental.pallas import tpu as pltpu
from jax.sharding import PartitionSpec as P

EPS = 1e-06
CAP = 30.0
MESH = pl.DeviceIdType.MESH
ANY = pl.BlockSpec(memory_space=pl.ANY)
VMEM = pl.BlockSpec(memory_space=pltpu.VMEM)
CONTRACT_LAST = (((1,), (1,)), ((), ()))
CONTRACT_FIRST = (((0,), (0,)), ((), ()))
W_CHUNK = 32
BACK_CHUNKS = 4


def position():
    return lax.axis_index("pipe"), lax.axis_index("tensor"), lax.axis_index("dp")


def remote(src, dst, send_sem, recv_sem, device):
    return pltpu.make_async_remote_copy(
        src_ref=src,
        dst_ref=dst,
        send_sem=send_sem,
        recv_sem=recv_sem,
        device_id=device,
        device_id_type=MESH,
    )


def signal(sem, device):
    pl.semaphore_signal(sem, inc=1, device_id=device, device_id_type=MESH)


def greet_pipe(barrier, n_pipe):
    p, t, j = position()

    @pl.loop(1, n_pipe)
    def _(k):
        signal(barrier, (lax.rem(p + k, n_pipe), t, j))


def greet_dp(barrier, n_dp):
    p, t, j = position()

    @pl.loop(1, n_dp)
    def _(k):
        signal(barrier, (p, t, lax.rem(j + k, n_dp)))


def gather_kernel(
    n_pipe, n_dp,
    w_ref, a_ref, gain_ref,
    w7_ref, a7_ref, g7_ref, all_ref,
    local_sem, w_recv, w_up, w_down, s_recv, s_send, g_recv, g_send,
    a_recv, a_send, v_recv, v_send, v_fwd,
):
    p, t, j = position()
    last = n_pipe - 1
    up_hops = n_pipe // 2
    down_hops = last - up_hops
    core = lax.rem(j, 2)
    sibling = j + 1 - 2 * core
    n_chips = n_dp // 2
    chip = j // 2
    chunks = w_ref.shape[0] // W_CHUNK
    is_last = p == last

    barrier = pltpu.get_barrier_semaphore()
    greet_pipe(barrier, n_pipe)
    greet_dp(barrier, n_dp)
    pl.semaphore_wait(barrier, n_pipe - 1 + n_dp - 1)

    def rows(ref, c):
        return ref.at[pl.ds(pl.multiple_of(c * W_CHUNK, W_CHUNK), W_CHUNK)]

    def slice_copy(q):
        return remote(a_ref.at[q], a7_ref.at[j], s_send.at[q], s_recv, (q, t, j))

    def gain_copy(q):
        return remote(gain_ref, g7_ref, g_send.at[q], g_recv, (q, t, j))

    def weight_copy(source, c, sems, q):
        return remote(rows(source, c), rows(w7_ref, c), sems.at[c], w_recv.at[c], (q, t, j))

    up = lax.rem(p + 1, n_pipe)
    down = lax.rem(p + last, n_pipe)

    @pl.when(is_last)
    def _():
        pltpu.make_async_copy(a_ref.at[last], a7_ref.at[j], local_sem.at[0]).start()

        @pl.loop(0, last)
        def _(q):
            slice_copy(q).start()

        @pl.loop(0, chunks)
        def _(c):
            weight_copy(w_ref, c, w_up, up).start()
            if down_hops:
                weight_copy(w_ref, c, w_down, down).start()

        @pl.loop(0, last)
        def _(q):
            gain_copy(q).start()

        pltpu.make_async_copy(w_ref, w7_ref, local_sem.at[1]).start()
        pltpu.make_async_copy(gain_ref, g7_ref, local_sem.at[2]).start()

    own_values = pltpu.make_async_copy(a_ref, all_ref.at[:, j], local_sem.at[3])
    own_values.start()

    def values_copy(k):
        other = lax.rem(chip + k, n_chips) * 2 + core
        return remote(a_ref, all_ref.at[:, j], v_send.at[k], v_recv.at[j], (p, t, other))

    def forward_copy(k):
        owner = lax.rem(chip + n_chips - k, n_chips) * 2 + core
        return remote(
            all_ref.at[:, owner], all_ref.at[:, owner], v_fwd.at[k], v_recv.at[owner], (p, t, sibling)
        )

    def arrived_values(owner):
        return remote(a_ref, all_ref.at[:, owner], v_send.at[0], v_recv.at[owner], (p, t, sibling))

    own_pair = remote(a_ref, all_ref.at[:, j], v_send.at[0], v_recv.at[j], (p, t, sibling))

    @pl.when(is_last)
    def _():
        pltpu.make_async_copy(a_ref.at[last], a7_ref.at[j], local_sem.at[0]).wait()

    @pl.when(jnp.logical_not(is_last))
    def _():
        slice_copy(p).wait_recv()

    def token_copy(k):
        return remote(
            a7_ref.at[j], a7_ref.at[j], a_send.at[k], a_recv.at[j], (p, t, lax.rem(j + k, n_dp))
        )

    def arrived_tokens(owner):
        return remote(a7_ref.at[j], a7_ref.at[owner], a_send.at[0], a_recv.at[owner], (p, t, sibling))

    @pl.loop(1, n_dp)
    def _(k):
        token_copy(k).start()

    own_pair.start()

    @pl.loop(1, n_chips)
    def _(k):
        values_copy(k).start()

    @pl.when(p < last)
    def _():
        @pl.loop(0, chunks)
        def _(c):
            weight_copy(w_ref, c, w_up, up).wait_recv()

            @pl.when(p < up_hops - 1)
            def _():
                weight_copy(w7_ref, c, w_up, up).start()

            @pl.when(p > up_hops)
            def _():
                weight_copy(w7_ref, c, w_down, down).start()

    @pl.loop(1, n_chips)
    def _(k):
        arrived_values(lax.rem(chip + n_chips - k, n_chips) * 2 + core).wait_recv()
        forward_copy(k).start()

    @pl.loop(1, n_dp)
    def _(k):
        arrived_tokens(lax.rem(j + k, n_dp)).wait_recv()

    arrived_values(sibling).wait_recv()

    @pl.loop(1, n_chips)
    def _(k):
        arrived_values(lax.rem(chip + n_chips - k, n_chips) * 2 + 1 - core).wait_recv()

    @pl.loop(1, n_dp)
    def _(k):
        token_copy(k).wait_send()

    own_pair.wait_send()
    own_values.wait()

    @pl.loop(1, n_chips)
    def _(k):
        values_copy(k).wait_send()
        forward_copy(k).wait_send()

    @pl.when(is_last)
    def _():
        @pl.loop(0, last)
        def _(q):
            slice_copy(q).wait_send()
            gain_copy(q).wait_send()

        @pl.loop(0, chunks)
        def _(c):
            weight_copy(w_ref, c, w_up, up).wait_send()
            if down_hops:
                weight_copy(w_ref, c, w_down, down).wait_send()

        pltpu.make_async_copy(w_ref, w7_ref, local_sem.at[1]).wait()
        pltpu.make_async_copy(gain_ref, g7_ref, local_sem.at[2]).wait()

    @pl.when(jnp.logical_not(is_last))
    def _():
        gain_copy(p).wait_recv()

        @pl.when(p < up_hops - 1)
        def _():
            @pl.loop(0, chunks)
            def _(c):
                weight_copy(w7_ref, c, w_up, up).wait_send()

        @pl.when(p > up_hops)
        def _():
            @pl.loop(0, chunks)
            def _(c):
                weight_copy(w7_ref, c, w_down, down).wait_send()


def gather(weight, values, gain, n_pipe, n_dp):
    dma = pltpu.SemaphoreType.DMA
    chunks = weight.shape[0] // W_CHUNK
    tokens, width = values.shape[1:]
    kind = jnp.bfloat16
    return pl.pallas_call(
        functools.partial(gather_kernel, n_pipe, n_dp),
        out_shape=(
            jax.ShapeDtypeStruct(weight.shape, kind),
            jax.ShapeDtypeStruct((n_dp, tokens, width), kind),
            jax.ShapeDtypeStruct(gain.shape, jnp.float32),
            jax.ShapeDtypeStruct((n_pipe, n_dp, tokens, width), kind),
        ),
        in_specs=[ANY] * 3,
        out_specs=(ANY,) * 4,
        scratch_shapes=[
            dma((4,)),
            dma((chunks,)), dma((chunks,)), dma((chunks,)),
            dma, dma((n_pipe,)), dma, dma((n_pipe,)),
            dma((n_dp,)), dma((n_dp,)),
            dma((n_dp,)), dma((n_dp // 2,)), dma((n_dp // 2,)),
        ],
        compiler_params=pltpu.CompilerParams(collective_id=0, has_side_effects=True),
        name="gather_sections",
    )(weight, values, gain)


def normalize(value):
    scale = lax.rsqrt(jnp.mean(value * value, axis=-1, keepdims=True) + EPS)
    return scale, value * scale


def flatten(blocks):
    return jnp.concatenate(blocks, axis=1)


def head_kernel(
    n_pipe, n_dp,
    part_ref, embed_ref, input_ref, g7_ref, gain_ref, target_ref, rest_ref,
    tg_ref, delta_ref, hz_ref, tz_ref,
    embed, parts, sum_out, sum_in, back_out, back_in, block,
    embed_sem, p_recv, p_send, sum_sem, back_recv, back_send,
    d_recv, d_send, h_recv, h_send, z_recv, z_send,
    t_recv, t_send, r_recv, r_up, r_down, local_sem,
):
    p, t, j = position()
    last = n_pipe - 1
    up_hops = n_pipe // 2
    down_hops = last - up_hops
    other = 1 - t
    per_pipe = hz_ref.shape[1]
    tokens = part_ref.shape[1]
    width = part_ref.shape[2]
    vrows, model = embed_ref.shape

    load = pltpu.make_async_copy(embed_ref, embed, embed_sem)
    load.start()
    barrier = pltpu.get_barrier_semaphore()
    greet_dp(barrier, n_dp)

    @pl.loop(0, n_dp)
    def _(k):
        signal(barrier, (p, other, k))

    greet_pipe(barrier, n_pipe)
    pl.semaphore_wait(barrier, 2 * n_dp - 1 + n_pipe - 1)

    def same_copy(k):
        q = lax.rem(j + k, n_dp)
        return remote(part_ref.at[q], parts.at[t, j], p_send.at[0, k], p_recv.at[t, j], (p, t, q))

    def cross_copy(k):
        q = lax.rem(j + k, n_dp)
        return remote(part_ref.at[q], parts.at[t, j], p_send.at[1, k], p_recv.at[t, j], (p, other, q))

    own_part = pltpu.make_async_copy(part_ref.at[j], parts.at[t, j], local_sem.at[0])
    own_part.start()

    @pl.loop(0, n_dp)
    def _(k):
        cross_copy(k).start()

    @pl.loop(1, n_dp)
    def _(k):
        same_copy(k).start()

    def arrived(group, q):
        return remote(part_ref.at[q], parts.at[group, q], p_send.at[0, 0], p_recv.at[group, q], (p, other, j))

    own_part.wait()

    @pl.loop(0, n_dp)
    def _(k):
        arrived(other, k).wait_recv()

    @pl.loop(1, n_dp)
    def _(k):
        arrived(t, lax.rem(j + k, n_dp)).wait_recv()

    output = flatten(
        [parts[0, q].astype(jnp.float32) + parts[1, q].astype(jnp.float32) for q in range(n_dp)]
    )
    _, normed = normalize(output)
    mine = pl.ds(pl.multiple_of(p * tokens, tokens), tokens)
    resid = input_ref[mine, :].astype(jnp.float32) + normed * g7_ref[...]
    y_scale, y_normed = normalize(resid)
    head_in = (y_normed * gain_ref[...]).astype(jnp.bfloat16)

    for b in range(n_dp):
        block[0, b] = head_in[:, b * width:(b + 1) * width]

    def line_copy(slot, out_ref, send, recv, k):
        q = lax.rem(p + k, n_pipe)
        return remote(
            block.at[slot, pl.ds(q * per_pipe, per_pipe)], out_ref.at[p], send.at[k], recv.at[p], (q, t, j)
        )

    def line_arrived(slot, out_ref, send, recv, q):
        return remote(
            block.at[slot, pl.ds(0, per_pipe)], out_ref.at[q], send.at[0], recv.at[q], (q, t, j)
        )

    own_head = pltpu.make_async_copy(
        block.at[0, pl.ds(p * per_pipe, per_pipe)], hz_ref.at[p], local_sem.at[1]
    )
    own_head.start()

    @pl.loop(1, n_pipe)
    def _(k):
        line_copy(0, hz_ref, h_send, h_recv, k).start()

    load.wait()
    raw = lax.dot_general(head_in, embed[...], CONTRACT_LAST, preferred_element_type=jnp.float32)
    capped = jnp.tanh(raw / CAP)
    logits = CAP * capped
    own_sum = jnp.sum(jnp.exp(logits), axis=1, keepdims=True)
    sum_out[...] = jnp.broadcast_to(own_sum, sum_out.shape)
    pair = (p, other, j)
    sums = remote(sum_out, sum_in, sum_sem.at[0], sum_sem.at[1], pair)
    sums.start()
    column = lax.broadcasted_iota(jnp.int32, (tokens, vrows), 1)
    hit = (target_ref[mine, :] - t * vrows == column).astype(jnp.float32)
    slope = 1.0 - capped * capped
    sums.wait_recv()
    log_total = jnp.log(own_sum + sum_in[:, 0:1])
    rest = rest_ref[mine, :]
    high = jnp.maximum(rest, log_total)
    lse = high + jnp.log(1.0 + jnp.exp(-jnp.abs(rest - log_total)))
    delta = ((jnp.exp(logits - lse) - hit) * slope).astype(jnp.bfloat16)

    sum_out_delta = back_out.at[BACK_CHUNKS, :, pl.ds(0, vrows)]
    sum_out_delta[...] = delta
    own_delta = pltpu.make_async_copy(sum_out_delta, delta_ref.at[p], local_sem.at[2])
    own_delta.start()

    def delta_copy(k):
        q = lax.rem(p + k, n_pipe)
        return remote(sum_out_delta, delta_ref.at[p], d_send.at[k], d_recv.at[p], (q, t, j))

    def delta_arrived(q):
        return remote(sum_out_delta, delta_ref.at[q], d_send.at[0], d_recv.at[q], (q, t, j))

    @pl.loop(1, n_pipe)
    def _(k):
        delta_copy(k).start()

    step = model // BACK_CHUNKS
    copies = []
    for c in range(BACK_CHUNKS):
        piece = jnp.dot(delta, embed[:, c * step:(c + 1) * step], preferred_element_type=jnp.float32)
        back_out[c, :, 0:step] = piece.astype(jnp.bfloat16)
        copy = remote(
            back_out.at[c, :, pl.ds(0, step)], back_in.at[c], back_send.at[c], back_recv.at[c], pair
        )
        copy.start()
        copies.append(copy)
    grads = []
    for c in range(BACK_CHUNKS):
        copies[c].wait_recv()
        grads.append(back_out[c, :, 0:step].astype(jnp.float32) + back_in[c].astype(jnp.float32))
    grad = flatten(grads) * gain_ref[...]
    top = y_scale * (grad - y_normed * jnp.mean(grad * y_normed, axis=-1, keepdims=True))
    top = top.astype(jnp.bfloat16)
    for b in range(n_dp):
        block[1, b] = top[:, b * width:(b + 1) * width]

    def column_copy(k):
        q = lax.rem(j + k, n_dp)
        return remote(block.at[1, q], tg_ref.at[p, j], t_send.at[k], t_recv.at[j], (p, t, q))

    def column_arrived(q):
        return remote(block.at[1, q], tg_ref.at[p, q], t_send.at[0], t_recv.at[q], pair)

    own_column = pltpu.make_async_copy(block.at[1, j], tg_ref.at[p, j], local_sem.at[3])
    own_column.start()

    @pl.loop(1, n_dp)
    def _(k):
        column_copy(k).start()

    own_top = pltpu.make_async_copy(
        block.at[1, pl.ds(p * per_pipe, per_pipe)], tz_ref.at[p], local_sem.at[4]
    )
    own_top.start()

    @pl.loop(1, n_pipe)
    def _(k):
        line_copy(1, tz_ref, z_send, z_recv, k).start()

    own_column.wait()

    @pl.loop(1, n_dp)
    def _(k):
        column_arrived(lax.rem(j + k, n_dp)).wait_recv()

    up = (lax.rem(p + 1, n_pipe), t, j)
    down = (lax.rem(p + last, n_pipe), t, j)

    def ring_copy(plane, send, device):
        return remote(tg_ref.at[plane], tg_ref.at[plane], send.at[plane], r_recv.at[plane], device)

    def above(s):
        return lax.rem(p + s, n_pipe)

    def below(s):
        return lax.rem(p + n_pipe - s, n_pipe)

    for s in range(up_hops + 1):
        if s > 0:
            ring_copy(below(s), r_up, up).wait_recv()
        if s < up_hops:
            ring_copy(below(s), r_up, up).start()
        if 0 < s <= down_hops:
            ring_copy(above(s), r_down, down).wait_recv()
        if s < down_hops:
            ring_copy(above(s), r_down, down).start()

    own_head.wait()
    own_delta.wait()
    own_top.wait()

    @pl.loop(1, n_pipe)
    def _(k):
        q = lax.rem(p + k, n_pipe)
        line_arrived(0, hz_ref, h_send, h_recv, q).wait_recv()
        line_arrived(1, tz_ref, z_send, z_recv, q).wait_recv()
        delta_arrived(q).wait_recv()
        line_copy(0, hz_ref, h_send, h_recv, k).wait_send()
        line_copy(1, tz_ref, z_send, z_recv, k).wait_send()
        delta_copy(k).wait_send()

    @pl.loop(0, n_dp)
    def _(k):
        cross_copy(k).wait_send()

    @pl.loop(1, n_dp)
    def _(k):
        same_copy(k).wait_send()
        column_copy(k).wait_send()

    sums.wait_send()
    for copy in copies:
        copy.wait_send()
    for s in range(up_hops):
        ring_copy(below(s), r_up, up).wait_send()
    for s in range(down_hops):
        ring_copy(above(s), r_down, down).wait_send()


def head(part, embed, section_input, g7, final_gain, target, rest, n_pipe, n_dp):
    dma = pltpu.SemaphoreType.DMA
    _, tokens, width = part.shape
    vrows, model = embed.shape
    per_pipe = n_dp // n_pipe
    step = model // BACK_CHUNKS
    kind = jnp.bfloat16
    return pl.pallas_call(
        functools.partial(head_kernel, n_pipe, n_dp),
        out_shape=(
            jax.ShapeDtypeStruct((n_pipe, n_dp, tokens, width), kind),
            jax.ShapeDtypeStruct((n_pipe, tokens, vrows), kind),
            jax.ShapeDtypeStruct((n_pipe, per_pipe, tokens, width), kind),
            jax.ShapeDtypeStruct((n_pipe, per_pipe, tokens, width), kind),
        ),
        in_specs=[VMEM, ANY, VMEM, VMEM, VMEM, VMEM, VMEM],
        out_specs=(ANY,) * 4,
        scratch_shapes=[
            pltpu.VMEM((vrows, model), kind),
            pltpu.VMEM((2, n_dp, tokens, width), kind),
            pltpu.VMEM((tokens, 128), jnp.float32),
            pltpu.VMEM((tokens, 128), jnp.float32),
            pltpu.VMEM((BACK_CHUNKS + 1, tokens, max(step, vrows)), kind),
            pltpu.VMEM((BACK_CHUNKS, tokens, step), kind),
            pltpu.VMEM((2, n_dp, tokens, width), kind),
            dma, dma((2, n_dp)), dma((2, n_dp)), dma((2,)), dma((BACK_CHUNKS,)), dma((BACK_CHUNKS,)),
            dma((n_pipe,)), dma((n_pipe,)), dma((n_pipe,)), dma((n_pipe,)), dma((n_pipe,)), dma((n_pipe,)),
            dma((n_dp,)), dma((n_dp,)), dma((n_pipe,)), dma((n_pipe,)), dma((n_pipe,)), dma((5,)),
        ],
        compiler_params=pltpu.CompilerParams(
            collective_id=1, has_side_effects=True, vmem_limit_bytes=40 * 1024 * 1024
        ),
        cost_estimate=pl.CostEstimate(flops=40_000_000_000, bytes_accessed=100_000_000, transcendentals=0),
        name="head_block",
    )(part, embed, section_input, g7, final_gain, target, rest)


def exchange_kernel(
    n_dp, term_ref, stat_ref, terms_ref, stats_ref, t_recv, t_send, s_recv, s_send, local_sem
):
    p, t, j = position()
    barrier = pltpu.get_barrier_semaphore()
    greet_dp(barrier, n_dp)
    pl.semaphore_wait(barrier, n_dp - 1)

    def stat_copy(k):
        return remote(stat_ref, stats_ref.at[j], s_send.at[k], s_recv.at[j], (p, t, lax.rem(j + k, n_dp)))

    def term_copy(k):
        q = lax.rem(j + k, n_dp)
        return remote(term_ref.at[:, q], terms_ref.at[j], t_send.at[k], t_recv.at[j], (p, t, q))

    def stat_arrived(q):
        return remote(stat_ref, stats_ref.at[q], s_send.at[0], s_recv.at[q], (p, t, q))

    def term_arrived(q):
        return remote(term_ref.at[:, q], terms_ref.at[q], t_send.at[0], t_recv.at[q], (p, t, q))

    @pl.loop(1, n_dp)
    def _(k):
        stat_copy(k).start()

    @pl.loop(1, n_dp)
    def _(k):
        term_copy(k).start()

    own_stat = pltpu.make_async_copy(stat_ref, stats_ref.at[j], local_sem.at[0])
    own_term = pltpu.make_async_copy(term_ref.at[:, j], terms_ref.at[j], local_sem.at[1])
    own_stat.start()
    own_term.start()
    own_stat.wait()
    own_term.wait()

    @pl.loop(1, n_dp)
    def _(k):
        q = lax.rem(j + k, n_dp)
        stat_arrived(q).wait_recv()
        term_arrived(q).wait_recv()
        stat_copy(k).wait_send()
        term_copy(k).wait_send()


def exchange(term, stat, n_dp):
    dma = pltpu.SemaphoreType.DMA
    groups, _, rows, width = term.shape
    return pl.pallas_call(
        functools.partial(exchange_kernel, n_dp),
        out_shape=(
            jax.ShapeDtypeStruct((n_dp, groups, rows, width), term.dtype),
            jax.ShapeDtypeStruct((n_dp,) + stat.shape, stat.dtype),
        ),
        in_specs=[ANY] * 2,
        out_specs=(ANY,) * 2,
        scratch_shapes=[dma((n_dp,)), dma((n_dp,)), dma((n_dp,)), dma((n_dp,)), dma((2,))],
        compiler_params=pltpu.CompilerParams(collective_id=2, has_side_effects=True),
        name="exchange_terms",
    )(term, stat)


def per_device(
    section_proj,
    attn_values,
    post_gain,
    section_input,
    final_gain,
    embed_block,
    token_ids,
    target_ids,
    block_offset,
    rest_lse,
):
    n_pipe, n_dp = lax.axis_size("pipe"), lax.axis_size("dp")
    weight = section_proj[0]
    width, depth = weight.shape
    model = section_input.shape[2]
    vrows = embed_block.shape[0]
    count = section_input.shape[0] * section_input.shape[1]
    tokens = count // n_pipe
    values = attn_values.reshape(n_pipe, tokens, depth)
    every = n_pipe * n_dp * tokens

    w7, a7, g7, gathered = gather(weight, values, post_gain, n_pipe, n_dp)
    part = lax.dot_general(
        a7.reshape(n_dp * tokens, depth), w7, CONTRACT_LAST, preferred_element_type=jnp.float32
    ).astype(jnp.bfloat16)
    gathered = gathered.reshape(every, depth)
    own_part = lax.dot_general(
        gathered, weight, CONTRACT_LAST, preferred_element_type=jnp.float32
    ).astype(jnp.bfloat16)
    part, own_part = lax.optimization_barrier((part, own_part))
    pair_part = lax.ppermute(own_part, "tensor", [(0, 1), (1, 0)])
    top, delta, head_cols, top_cols = head(
        part.reshape(n_dp, tokens, width),
        embed_block,
        section_input.reshape(count, model),
        g7,
        final_gain.reshape(1, model),
        target_ids.reshape(count, 1) - block_offset[0],
        rest_lse.reshape(count, 1),
        n_pipe,
        n_dp,
    )

    first_row = block_offset[0] + lax.axis_index("tensor") * vrows
    column = lax.broadcasted_iota(jnp.int32, (count, vrows), 1)
    used = (token_ids.reshape(count, 1) - first_row == column).astype(jnp.bfloat16)
    delta = delta.reshape(count, vrows)
    terms = []
    for b in range(n_dp // n_pipe):
        head_term = lax.dot_general(
            delta, head_cols[:, b].reshape(count, width), CONTRACT_FIRST, preferred_element_type=jnp.float32
        )
        embed_term = math.sqrt(model) * lax.dot_general(
            used, top_cols[:, b].reshape(count, width), CONTRACT_FIRST, preferred_element_type=jnp.float32
        )
        terms.append((head_term + embed_term).astype(jnp.bfloat16).reshape(n_dp, vrows // n_dp, width))
    term = jnp.stack(terms)

    output = own_part.astype(jnp.float32) + pair_part.astype(jnp.float32)
    own = lax.axis_index("dp") * width
    gain = lax.dynamic_slice(post_gain, (0, own), (1, width))
    grad = top.reshape(every, width).astype(jnp.float32) * gain
    stat = jnp.stack([jnp.sum(output * output, axis=1), jnp.sum(output * grad, axis=1)])
    terms, stats = exchange(term, stat.reshape(2 * every // 128, 128), n_dp)
    tied = jnp.sum(terms.astype(jnp.float32), axis=0)
    tied = jnp.concatenate([tied[b] for b in range(n_dp // n_pipe)], axis=1)
    square, cross = jnp.sum(stats, axis=0).reshape(2, every)
    scale = lax.rsqrt(square / model + EPS)
    out_grad = scale[:, None] * (grad - output * (scale * scale * cross / model)[:, None])
    own_grad = lax.dot_general(
        out_grad.astype(jnp.bfloat16), gathered, CONTRACT_FIRST, preferred_element_type=jnp.float32
    )
    return (own_grad[None], tied)


def solution(mesh):
    in_specs = (
        P("pipe", "dp", "tensor"),
        P("pipe", None, "dp", "tensor"),
        P("pipe", None),
        P(None, "dp", None),
        P(),
        P("tensor", None),
        P(None, "dp"),
        P(None, "dp"),
        P(),
        P(None, "dp"),
    )
    out_specs = (P("pipe", "dp", "tensor"), P(("tensor", "dp"), "pipe"))
    return jax.shard_map(
        per_device, mesh=mesh, in_specs=in_specs, out_specs=out_specs, check_vma=False
    )
```

time: 617 us -> 188 us (0.30)
  waiting for transfers between devices: 532 us -> 0.01 us
  Pallas kernels: 0 us -> 148 us
  matrix products: 46.3 us -> 14.8 us
  between operations: 14.9 us -> 1.54 us
  local copies, waits for them, and re-layouts: 4.95 us -> 12.2 us
    reduce_scatter x2 -> x0, waiting for transfers between devices: 225 us -> none  [the longest x1 116 us: per_device(): lax.psum_scatter(lax.dot_general(out_grad, values, contract_first, prefer...]
    psum x3 -> x0, waiting for transfers between devices: 182 us -> none  [the longest x1 73.6 us: broadcast(): return lax.psum(block, axis)]
    pallas_call x0 -> x3, Pallas kernels: none -> 148 us  [the longest x1 68.4 us: head(): pl.pallas_call(functools.partial(head_kernel, n_pipe, n_dp), out_shape=(j...]
    all_gather x1 -> x0, waiting for transfers between devices: 89.5 us -> none  [per_device(): lax.all_gather(weight, 'dp', axis=0, tiled=True)]
    unnamed x8 -> x0, waiting for transfers between devices: 35.8 us -> none
    dot_general x6 -> x7, matrix products: 46.3 us -> 14.8 us  [the longest x1 5.4 us: per_device(): lax.dot_general(out_grad.astype(jnp.bfloat16), gathered, CONTRACT_FIRST,...]
  transfers between devices with their start and end apart: 7 -> 1, of which waited for: 7 -> 0; matrix products, arithmetic and copies ran while one was open for 2% -> 9% of each run, Pallas kernels for 0% -> 37%
where the time goes in v1:
time: 188 us; the launch traced here: 187 us
  Pallas kernels  148 us (79%)
  matrix products  14.8 us (8%)
  local copies, waits for them, and re-layouts  12.2 us (6%)
  other arithmetic  10.4 us (6%)
    pallas_call x1, Pallas kernels, head(): pl.pallas_call(functools.partial(head_kernel, n_pipe, n_dp), out_shape=(j...  68.4 us
    pallas_call x1, Pallas kernels, gather(): pl.pallas_call(functools.partial(gather_kernel, n_pipe, n_dp), out_shape=...  49.2 us
    pallas_call x1, Pallas kernels, exchange(): pl.pallas_call(functools.partial(exchange_kernel, n_dp), out_shape=(jax.S...  30.2 us
    dot_general x1, matrix products, per_device(): lax.dot_general(out_grad.astype(jnp.bfloat16), gathered, CONTRACT_FIRST,...  5.4 us
    dot_general x1, matrix products, per_device(): lax.dot_general(gathered, weight, CONTRACT_LAST, preferred_element_type=j...  4.9 us
  transfers between devices with their start and end apart: 1, of which 0 were waited for; matrix products, arithmetic and copies ran while one was open for 9% of the time, Pallas kernels for 37%

profile of v1, /device:TPU:1, one launch (start us, length us, event | category | flops | bytes accessed | tf_op | source)
XLA Modules:
  0.0 187.3 jit_solution(3562283228112405457)
XLA Ops:
  0.6 49.2 %gather_sections.1 = (bf16[288,1024]{1,0:T(8,128)(2,1)}, bf16[16,16,1024]{2,1,0:T(8,128)(2,1)}, f32[1,4608]{1,0:T(1,128)}, bf16[8,16,16,1024]{3,2,1,0:T(8,128)(2,1)}) custom-call(bf16[288,1024]{1,0:T(8,128)(2,1)} %bitcast.55, bf16[8,16,1024]{2,1,0:T(8,128)(2,1)} %bitcast.61, f32[1,4608]{1,0:T(1,128)} %gain_ref.1), custom_call_target="tpu_custom_call" | custom-call | tf_op jit(solution)/shard_map/gather_sections/pallas_call | solution.py:239
  49.8 4.9 %convolution_convert_fusion = bf16[2048,288]{0,1:T(8,128)(2,1)} fusion(bf16[2048,1024]{1,0:T(8,128)(2,1)} %bitcast.64, bf16[1,288,1024]{2,1,0:T(8,128)(2,1)} %param.10), kind=kOutput, calls=%fused_computation.1 | convolution fusion | flops 1208549376 | bytes 5963776 | tf_op jit(solution)/shard_map/dot_general | solution.py:629
  54.8 0.4 convolution_convert_fusion.1
  55.1 0.6 collective-permute-start
  56.9 3.7 %copy-done = bf16[1024,4608]{1,0:T(8,128)(2,1)S(1)} copy-done((bf16[1024,4608]{1,0:T(8,128)(2,1)S(1)}, bf16[1024,4608]{1,0:T(8,128)(2,1)}, u32[]{:S(2)}) %copy-start) | copy-done | bytes 9437208
  60.6 68.4 %head_block.1 = (bf16[8,16,16,288]{3,2,1,0:T(8,128)(2,1)S(1)}, bf16[8,16,1024]{2,1,0:T(8,128)(2,1)S(1)}, bf16[8,2,16,288]{3,2,1,0:T(8,128)(2,1)S(1)}, bf16[8,2,16,288]{3,2,1,0:T(8,128)(2,1)S(1)}) custom-call(bf16[16,16,288]{2,1,0:T(8,128)(2,1)S(1)} %bitcast.51, bf16[1024,4608]{1,0:T(8,128)(2,1)S(1)} %copy-done, bf16[128,4608]{1,0:T(8,128)(2,1)S(1)} %bitcast.52, ...), custom_call_target="tpu_custom_call" | custom-call | flops 40000000000 | bytes 100000000 | tf_op jit(solution)/shard_map/head_block/pallas_call | solution.py:510
  129.0 2.0 %bitcast_convert_fusion = f32[2048,288]{1,0:T(8,128)} fusion(bf16[8,16,16,288]{3,2,1,0:T(8,128)(2,1)S(1)} %get-tuple-element.23), kind=kLoop, calls=%fused_computation.7 | loop fusion | flops 589824 | bytes 3538944 | tf_op jit(solution)/shard_map/convert_element_type | solution.py:664
  131.0 2.3 %copy.17 = f32[2048,288]{0,1:T(8,128)S(1)} copy(f32[2048,288]{1,0:T(8,128)} %bitcast_convert_fusion) | data formatting | bytes 4718592 | tf_op jit(solution)/shard_map/convert_element_type | solution.py:664
  133.5 0.7 fusion.15
  134.1 0.4 fusion.17
  134.5 1.2 fusion.2
  135.7 1.4 copy.15
  137.2 1.2 fusion.18
  138.4 1.3 fusion.3
  139.7 2.2 %copy.16 = bf16[1024,288]{1,0:T(8,128)(2,1)} copy(bf16[1024,288]{0,1:T(8,128)(2,1)} %fusion.3) | data formatting | bytes 1179648 | tf_op jit(solution)/shard_map/convert_element_type | solution.py:658
  141.9 0.8 dynamic-slice_reduce_fusion
  142.7 2.6 %pad_maximum_fusion.term_ref = bf16[2,16,64,288]{3,2,1,0:T(8,128)(2,1)} fusion(bf16[1,16,64,288]{3,2,1,0:T(8,128)(2,1)} %bitcast.54, bf16[1,16,64,288]{3,2,1,0:T(8,128)(2,1)S(1)} %bitcast.53), kind=kLoop, calls=%fused_computation.6 | loop fusion | flops 589824 | bytes 2359296 | tf_op jit(solution)/shard_map/stack | solution.py:659
  145.3 2.3 %multiply_reduce_fusion.1 = (f32[2048]{0:T(1024)S(1)}, f32[2048]{0:T(1024)S(1)}) fusion(bf16[2048,288]{0,1:T(8,128)(2,1)} %collective-permute-done, bf16[2048,288]{0,1:T(8,128)(2,1)} %convolution_convert_fusion, f32[2048,288]{0,1:T(8,128)S(1)} %copy.17, f32[288]{0:T(512)S(1)} %dynamic-slice_reduce_fusion), kind=kLoop, calls=%fused_computation.4 | loop fusion | flops 4714496 | bytes 4736128 | tf_op jit(solution)/shard_map/reduce_sum | solution.py:665
  147.6 0.6 reshape.94.stat_ref
  148.2 30.2 %exchange_terms.1 = (bf16[16,2,64,288]{3,2,1,0:T(8,128)(2,1)}, f32[16,32,128]{2,1,0:T(8,128)}) custom-call(bf16[2,16,64,288]{3,2,1,0:T(8,128)(2,1)} %pad_maximum_fusion.term_ref, f32[32,128]{1,0:T(8,128)} %reshape.94.stat_ref), custom_call_target="tpu_custom_call" | custom-call | tf_op jit(solution)/shard_map/exchange_terms/pallas_call | solution.py:588
  178.4 1.0 reduce_sum.38
  179.4 1.7 convert_reduce_fusion
  181.1 0.8 pad_maximum_fusion.1
  181.9 5.4 %convolution_bitcast_fusion = f32[1,288,1024]{2,1,0:T(8,128)} fusion(bf16[2048,1024]{1,0:T(8,128)(2,1)} %bitcast.65, f32[2048,288]{0,1:T(8,128)S(1)} %copy.17, bf16[2048,288]{0,1:T(8,128)(2,1)} %collective-permute-done, bf16[2048,288]{0,1:T(8,128)(2,1)} %convolution_convert_fusion, f32[2048]{0:T(1024)S(1)} %fusion.10, f32[2048]{0:T(1024)S(1)} %fusion.13, ...), kind=kOutput, calls=%fused_computation.12 | convolution fusion | flops 1212678144 | bytes 10110080 | tf_op jit(solution)/shard_map/dot_general | solution.py:672
  (29 shorter events, 0.6 us)
Async XLA Ops:
  49.8 5.0 %copy-start.3 = (bf16[288,1024]{1,0:T(8,128)(2,1)S(1)}, bf16[288,1024]{1,0:T(8,128)(2,1)}, u32[]{:S(2)}) copy-start(bf16[288,1024]{1,0:T(8,128)(2,1)} %get-tuple-element.15) | copy-start | bytes 1769476
  49.8 5.0 %copy-start.4 = (bf16[16,16,1024]{2,1,0:T(8,128)(2,1)S(1)}, bf16[16,16,1024]{2,1,0:T(8,128)(2,1)}, u32[]{:S(2)}) copy-start(bf16[16,16,1024]{2,1,0:T(8,128)(2,1)} %get-tuple-element.14) | copy-start | bytes 1572868
  54.7 1.8 copy-start.7
  54.7 2.0 %copy-start.6 = (f32[4,32]{1,0:T(4,128)S(1)}, f32[4,32]{1,0:T(4,128)}, u32[]{:S(2)}) copy-start(f32[4,32]{1,0:T(4,128)} %param.19) | copy-start | bytes 1540
  54.7 2.1 %copy-start.5 = (f32[4608]{0:T(1024)S(1)}, f32[4608]{0:T(1024)}, u32[]{:S(2)}) copy-start(f32[4608]{0:T(1024)} %param.14) | copy-start | bytes 55300
  54.7 2.1 %copy-start.1 = (bf16[4,32,4608]{2,1,0:T(8,128)(2,1)S(1)}, bf16[4,32,4608]{2,1,0:T(8,128)(2,1)}, u32[]{:S(2)}) copy-start(bf16[4,32,4608]{2,1,0:T(8,128)(2,1)} %param.13) | copy-start | bytes 3538948
  54.7 2.1 %copy-start.2 = (f32[1,4608]{1,0:T(1,128)S(1)}, f32[1,4608]{1,0:T(1,128)}, u32[]{:S(2)}) copy-start(f32[1,4608]{1,0:T(1,128)} %get-tuple-element.18.g7_ref) | copy-start | bytes 55300
  55.1 90.1 %collective-permute-start = (bf16[2048,288]{0,1:T(8,128)(2,1)}, bf16[2048,288]{0,1:T(8,128)(2,1)}, u32[]{:S(2)}, u32[]{:S(2)}) collective-permute-start(bf16[2048,288]{0,1:T(8,128)(2,1)} %convolution_convert_fusion), channel_id=1, source_target_pairs={{0,16},{16,0},{1,17},{17,1},{2,18},{18,2},{3,19},{19,3},{4,20},{20... | collective-permute-start | bytes 3538952 | tf_op jit(solution)/shard_map/ppermute | solution.py:633
  56.9 3.7 %copy-start = (bf16[1024,4608]{1,0:T(8,128)(2,1)S(1)}, bf16[1024,4608]{1,0:T(8,128)(2,1)}, u32[]{:S(2)}) copy-start(bf16[1024,4608]{1,0:T(8,128)(2,1)} %embed_ref.1) | copy-start | bytes 28311556
  131.0 2.4 %copy-start.8 = (s32[4,32]{1,0:T(4,128)S(1)}, s32[4,32]{1,0:T(4,128)}, u32[]{:S(2)}) copy-start(s32[4,32]{1,0:T(4,128)} %param.16) | copy-start | bytes 1540

commit v2 on v0

v2 whole, which is shorter than its diff:
```python
import functools
import math

import jax
import jax.numpy as jnp
from jax import lax
from jax.experimental import pallas as pl
from jax.experimental.pallas import tpu as pltpu
from jax.sharding import PartitionSpec as P

EPS = 1e-06
CAP = 30.0
MESH = pl.DeviceIdType.MESH
ANY = pl.BlockSpec(memory_space=pl.ANY)
VMEM = pl.BlockSpec(memory_space=pltpu.VMEM)
CONTRACT_LAST = (((1,), (1,)), ((), ()))
W_CHUNK = 32
BACK_CHUNKS = 4
RING_CHUNKS = 3


def position():
    return lax.axis_index("pipe"), lax.axis_index("tensor"), lax.axis_index("dp")


def remote(src, dst, send_sem, recv_sem, device):
    return pltpu.make_async_remote_copy(
        src_ref=src,
        dst_ref=dst,
        send_sem=send_sem,
        recv_sem=recv_sem,
        device_id=device,
        device_id_type=MESH,
    )


def signal(sem, device):
    pl.semaphore_signal(sem, inc=1, device_id=device, device_id_type=MESH)


def greet_pipe(barrier, n_pipe):
    p, t, j = position()

    @pl.loop(1, n_pipe)
    def _(k):
        signal(barrier, (lax.rem(p + k, n_pipe), t, j))


def greet_dp(barrier, n_dp):
    p, t, j = position()

    @pl.loop(1, n_dp)
    def _(k):
        signal(barrier, (p, t, lax.rem(j + k, n_dp)))


def normalize(value):
    scale = lax.rsqrt(jnp.mean(value * value, axis=-1, keepdims=True) + EPS)
    return scale, value * scale


def flatten(blocks):
    return jnp.concatenate(blocks, axis=1)


def section_kernel(
    n_pipe, n_dp,
    w_ref, a_ref, gain_ref, embed_ref, input_ref, fgain_ref, target_ref, rest_ref, ids_ref, column_ref,
    proj_ref, tied_ref,
    embed, w, w7, a7, g7, every, rows_in, part, parts, sum_out, sum_in, delta_out, delta_all,
    back_out, back_in, block, hz, tz, col, tg, ps, ps_in, term, terms, stat, stats, coef,
    l_sem, w_recv, w_up, w_down, s_recv, s_send, g_recv, g_send, a_recv, a_send, v_recv, v_send, v_fwd,
    p_recv, p_send, sum_sem, back_recv, back_send, d_recv, d_send, h_recv, h_send, z_recv, z_send,
    c_recv, c_send, r_recv, r_up, r_down, o_recv, o_send, t_recv, t_send, st_recv, st_send,
):
    p, t, j = position()
    last = n_pipe - 1
    up_hops = n_pipe // 2
    down_hops = last - up_hops
    other = 1 - t
    core = lax.rem(j, 2)
    sibling = j + 1 - 2 * core
    n_chips = n_dp // 2
    chip = j // 2
    chunks = w_ref.shape[0] // W_CHUNK
    is_last = p == last
    up = (lax.rem(p + 1, n_pipe), t, j)
    down = (lax.rem(p + last, n_pipe), t, j)
    pair = (p, other, j)
    tokens, width = part.shape[1:]
    vrows, model = embed.shape
    per_pipe = n_dp // n_pipe
    plane = n_dp * tokens
    depth = w.shape[1]
    mine = pl.ds(pl.multiple_of(p * tokens, tokens), tokens)

    def dp_at(k):
        return lax.rem(j + k, n_dp)

    def pipe_at(k):
        return lax.rem(p + k, n_pipe)

    load_embed = pltpu.make_async_copy(embed_ref, embed, l_sem.at[0])
    load_weight = pltpu.make_async_copy(w_ref, w, l_sem.at[1])
    load_rows = pltpu.make_async_copy(input_ref.at[mine], rows_in, l_sem.at[2])
    load_values = pltpu.make_async_copy(a_ref, every.at[:, j], l_sem.at[3])
    load_weight.start()
    load_rows.start()

    barrier = pltpu.get_barrier_semaphore()
    greet_pipe(barrier, n_pipe)
    greet_dp(barrier, n_dp)

    @pl.loop(0, n_dp)
    def _(k):
        signal(barrier, (p, other, k))

    pl.semaphore_wait(barrier, 2 * n_dp - 1 + n_pipe - 1)

    def piece(ref, c):
        return ref.at[pl.ds(pl.multiple_of(c * W_CHUNK, W_CHUNK), W_CHUNK)]

    def slice_copy(q):
        return remote(a_ref.at[q], a7.at[j], s_send.at[q], s_recv, (q, t, j))

    def gain_copy(q):
        return remote(gain_ref, g7, g_send.at[q], g_recv, (q, t, j))

    def weight_copy(source, c, sems, device):
        return remote(piece(source, c), piece(w7, c), sems.at[c], w_recv.at[c], device)

    own_slice = pltpu.make_async_copy(a_ref.at[last], a7.at[j], l_sem.at[4])
    own_weight = pltpu.make_async_copy(w_ref, w7, l_sem.at[5])
    own_gain = pltpu.make_async_copy(gain_ref, g7, l_sem.at[6])

    @pl.when(is_last)
    def _():
        own_slice.start()

        @pl.loop(0, last)
        def _(q):
            slice_copy(q).start()

        @pl.loop(0, chunks)
        def _(c):
            weight_copy(w_ref, c, w_up, up).start()
            if down_hops:
                weight_copy(w_ref, c, w_down, down).start()

        @pl.loop(0, last)
        def _(q):
            gain_copy(q).start()

        own_weight.start()
        own_gain.start()

    load_values.start()
    load_embed.start()

    def values_copy(k):
        q = lax.rem(chip + k, n_chips) * 2 + core
        return remote(a_ref, every.at[:, j], v_send.at[k], v_recv.at[j], (p, t, q))

    def behind(k):
        return lax.rem(chip + n_chips - k, n_chips) * 2

    def forward_copy(k):
        owner = behind(k) + core
        return remote(
            every.at[:, owner], every.at[:, owner], v_fwd.at[k], v_recv.at[owner], (p, t, sibling)
        )

    def values_arrived(owner):
        return remote(a_ref, every.at[:, owner], v_send.at[0], v_recv.at[owner], (p, t, sibling))

    own_values = remote(a_ref, every.at[:, j], v_send.at[0], v_recv.at[j], (p, t, sibling))

    @pl.when(is_last)
    def _():
        own_slice.wait()

    @pl.when(jnp.logical_not(is_last))
    def _():
        slice_copy(p).wait_recv()

    def token_copy(k):
        return remote(a7.at[j], a7.at[j], a_send.at[k], a_recv.at[j], (p, t, dp_at(k)))

    def tokens_arrived(q):
        return remote(a7.at[j], a7.at[q], a_send.at[0], a_recv.at[q], (p, t, sibling))

    @pl.loop(1, n_dp)
    def _(k):
        token_copy(k).start()

    own_values.start()

    @pl.loop(1, n_chips)
    def _(k):
        values_copy(k).start()

    @pl.when(is_last)
    def _():
        own_weight.wait()
        own_gain.wait()

    @pl.when(jnp.logical_not(is_last))
    def _():
        @pl.loop(0, chunks)
        def _(c):
            weight_copy(w_ref, c, w_up, up).wait_recv()

            @pl.when(p < up_hops - 1)
            def _():
                weight_copy(w7, c, w_up, up).start()

            @pl.when(p > up_hops)
            def _():
                weight_copy(w7, c, w_down, down).start()

        gain_copy(p).wait_recv()

    @pl.loop(1, n_dp)
    def _(k):
        tokens_arrived(dp_at(k)).wait_recv()

    part[...] = (
        lax.dot_general(
            a7[...].reshape(plane, depth), w7[...], CONTRACT_LAST, preferred_element_type=jnp.float32
        )
        .astype(jnp.bfloat16)
        .reshape(n_dp, tokens, width)
    )

    def same_copy(k):
        q = dp_at(k)
        return remote(part.at[q], parts.at[t, j], p_send.at[0, k], p_recv.at[t, j], (p, t, q))

    def cross_copy(k):
        q = dp_at(k)
        return remote(part.at[q], parts.at[t, j], p_send.at[1, k], p_recv.at[t, j], (p, other, q))

    def part_arrived(group, q):
        return remote(part.at[q], parts.at[group, q], p_send.at[0, 0], p_recv.at[group, q], pair)

    @pl.loop(0, n_dp)
    def _(k):
        cross_copy(k).start()

    @pl.loop(1, n_dp)
    def _(k):
        same_copy(k).start()

    parts[t, j] = part[j]

    @pl.loop(1, n_chips)
    def _(k):
        values_arrived(behind(k) + core).wait_recv()
        forward_copy(k).start()

    load_rows.wait()
    load_embed.wait()

    @pl.loop(0, n_dp)
    def _(k):
        part_arrived(other, k).wait_recv()

    @pl.loop(1, n_dp)
    def _(k):
        part_arrived(t, dp_at(k)).wait_recv()

    output = flatten(
        [parts[0, q].astype(jnp.float32) + parts[1, q].astype(jnp.float32) for q in range(n_dp)]
    )
    _, normed = normalize(output)
    resid = rows_in[...].astype(jnp.float32) + normed * g7[...]
    y_scale, y_normed = normalize(resid)
    head_in = (y_normed * fgain_ref[...]).astype(jnp.bfloat16)
    for b in range(n_dp):
        block[0, b] = head_in[:, b * width:(b + 1) * width]

    def line_copy(slot, dst, send, recv, k):
        q = pipe_at(k)
        return remote(
            block.at[slot, pl.ds(q * per_pipe, per_pipe)], dst.at[p], send.at[k], recv.at[p], (q, t, j)
        )

    def line_arrived(slot, dst, send, recv, q):
        return remote(block.at[slot, pl.ds(0, per_pipe)], dst.at[q], send.at[0], recv.at[q], (q, t, j))

    @pl.loop(1, n_pipe)
    def _(k):
        line_copy(0, hz, h_send, h_recv, k).start()

    for b in range(per_pipe):
        hz[p, b] = block[0, p * per_pipe + b]

    raw = lax.dot_general(head_in, embed[...], CONTRACT_LAST, preferred_element_type=jnp.float32)
    capped = jnp.tanh(raw / CAP)
    logits = CAP * capped
    own_sum = jnp.sum(jnp.exp(logits), axis=1, keepdims=True)
    sum_out[...] = jnp.broadcast_to(own_sum, sum_out.shape)
    sums = remote(sum_out, sum_in, sum_sem.at[0], sum_sem.at[1], pair)
    sums.start()
    lane = lax.broadcasted_iota(jnp.int32, (tokens, vrows), 1)
    hit = (target_ref[mine, :] - t * vrows == lane).astype(jnp.float32)
    slope = 1.0 - capped * capped
    sums.wait_recv()
    log_total = jnp.log(own_sum + sum_in[:, 0:1])
    rest = rest_ref[mine, :]
    lse = jnp.maximum(rest, log_total) + jnp.log(1.0 + jnp.exp(-jnp.abs(rest - log_total)))
    delta = ((jnp.exp(logits - lse) - hit) * slope).astype(jnp.bfloat16)
    delta_out[...] = delta
    delta_all[p] = delta

    step = model // BACK_CHUNKS
    copies = []
    for c in range(BACK_CHUNKS):
        grad = jnp.dot(delta, embed[:, c * step:(c + 1) * step], preferred_element_type=jnp.float32)
        back_out[c] = grad.astype(jnp.bfloat16)
        copy = remote(back_out.at[c], back_in.at[c], back_send.at[c], back_recv.at[c], pair)
        copy.start()
        copies.append(copy)

    def delta_copy(k):
        return remote(delta_out, delta_all.at[p], d_send.at[k], d_recv.at[p], (pipe_at(k), t, j))

    def delta_arrived(q):
        return remote(delta_out, delta_all.at[q], d_send.at[0], d_recv.at[q], (q, t, j))

    @pl.loop(1, n_pipe)
    def _(k):
        delta_copy(k).start()

    load_weight.wait()
    load_values.wait()
    values_arrived(sibling).wait_recv()

    @pl.loop(1, n_chips)
    def _(k):
        values_arrived(behind(k) + 1 - core).wait_recv()

    def output_copy(q):
        return remote(ps.at[q], ps_in.at[q], o_send.at[q], o_recv.at[q], pair)

    @pl.loop(0, n_pipe)
    def _(q):
        ps[q] = lax.dot_general(
            w[...], every[q].reshape(plane, depth), CONTRACT_LAST, preferred_element_type=jnp.float32
        ).astype(jnp.bfloat16)
        output_copy(q).start()

    grads = []
    for c in range(BACK_CHUNKS):
        copies[c].wait_recv()
        grads.append(back_out[c].astype(jnp.float32) + back_in[c].astype(jnp.float32))
    grad = flatten(grads) * fgain_ref[...]
    top = y_scale * (grad - y_normed * jnp.mean(grad * y_normed, axis=-1, keepdims=True))
    top = top.astype(jnp.bfloat16)
    for b in range(n_dp):
        block[1, b] = top[:, b * width:(b + 1) * width]

    def column_copy(k):
        q = dp_at(k)
        return remote(block.at[1, q], col.at[j], c_send.at[k], c_recv.at[j], (p, t, q))

    def column_arrived(q):
        return remote(block.at[1, q], col.at[q], c_send.at[0], c_recv.at[q], pair)

    @pl.loop(1, n_dp)
    def _(k):
        column_copy(k).start()

    @pl.loop(1, n_pipe)
    def _(k):
        line_copy(1, tz, z_send, z_recv, k).start()

    col[j] = block[1, j]
    for b in range(per_pipe):
        tz[p, b] = block[1, p * per_pipe + b]

    @pl.loop(1, n_dp)
    def _(k):
        column_arrived(dp_at(k)).wait_recv()

    tg[p] = col[...].reshape(plane, width).T

    ring_rows = width // RING_CHUNKS

    def ring_copy(source, c, send, device):
        ref = tg.at[source, pl.ds(c * ring_rows, ring_rows)]
        return remote(ref, ref, send.at[source, c], r_recv.at[source, c], device)

    def above(s):
        return lax.rem(p + s, n_pipe)

    def below(s):
        return lax.rem(p + n_pipe - s, n_pipe)

    for c in range(RING_CHUNKS):
        ring_copy(p, c, r_up, up).start()
        if down_hops:
            ring_copy(p, c, r_down, down).start()

    @pl.loop(1, n_pipe)
    def _(k):
        q = pipe_at(k)
        line_arrived(0, hz, h_send, h_recv, q).wait_recv()
        line_arrived(1, tz, z_send, z_recv, q).wait_recv()
        delta_arrived(q).wait_recv()

    count = n_pipe * tokens
    head_cols = flatten([hz[:, b].reshape(count, width) for b in range(per_pipe)])
    top_cols = flatten([tz[:, b].reshape(count, width) for b in range(per_pipe)])
    delta_rows = delta_all[...].reshape(count, vrows).T
    row = lax.broadcasted_iota(jnp.int32, (vrows, count), 0)
    used = (ids_ref[...] == row).astype(jnp.bfloat16)
    term[...] = (
        (
            jnp.dot(delta_rows, head_cols, preferred_element_type=jnp.float32)
            + math.sqrt(model) * jnp.dot(used, top_cols, preferred_element_type=jnp.float32)
        )
        .astype(jnp.bfloat16)
        .reshape(term.shape)
    )

    def term_copy(k):
        q = dp_at(k)
        return remote(term.at[q], terms.at[j], t_send.at[k], t_recv.at[j], (p, t, q))

    def term_arrived(q):
        return remote(term.at[q], terms.at[q], t_send.at[0], t_recv.at[q], pair)

    @pl.loop(1, n_dp)
    def _(k):
        term_copy(k).start()

    terms[j] = term[j]

    for s in range(1, up_hops + 1):
        for c in range(RING_CHUNKS):
            ring_copy(below(s), c, r_up, up).wait_recv()
            if s < up_hops:
                ring_copy(below(s), c, r_up, up).start()
            if s <= down_hops:
                ring_copy(above(s), c, r_down, down).wait_recv()
                if s < down_hops:
                    ring_copy(above(s), c, r_down, down).start()

    @pl.loop(0, n_pipe)
    def _(q):
        output_copy(q).wait_recv()
        out = ps[q].astype(jnp.float32) + ps_in[q].astype(jnp.float32)
        grad = tg[q].astype(jnp.float32) * column_ref[...]
        stat[pl.ds(q, 1), :] = jnp.sum(out * out, axis=0, keepdims=True)
        stat[pl.ds(n_pipe + q, 1), :] = jnp.sum(out * grad, axis=0, keepdims=True)

    def stat_copy(k):
        return remote(stat, stats.at[j], st_send.at[k], st_recv.at[j], (p, t, dp_at(k)))

    def stat_arrived(q):
        return remote(stat, stats.at[q], st_send.at[0], st_recv.at[q], pair)

    @pl.loop(1, n_dp)
    def _(k):
        stat_copy(k).start()

    stats[j] = stat[...]

    @pl.loop(1, n_dp)
    def _(k):
        term_arrived(dp_at(k)).wait_recv()

    total = terms[0].astype(jnp.float32)
    for q in range(1, n_dp):
        total = total + terms[q].astype(jnp.float32)
    tied_ref[...] = total

    @pl.loop(1, n_dp)
    def _(k):
        stat_arrived(dp_at(k)).wait_recv()

    both = jnp.sum(stats[...], axis=0)
    scale = lax.rsqrt(both[:n_pipe] / model + EPS)
    coef[0:n_pipe] = scale
    coef[n_pipe:2 * n_pipe] = scale * scale * both[n_pipe:] / model
    proj_ref[...] = jnp.zeros_like(proj_ref)

    @pl.loop(0, n_pipe)
    def _(q):
        out = ps[q].astype(jnp.float32) + ps_in[q].astype(jnp.float32)
        grad = tg[q].astype(jnp.float32) * column_ref[...]
        out_grad = coef[pl.ds(q, 1), :] * (grad - out * coef[pl.ds(n_pipe + q, 1), :])
        proj_ref[...] += jnp.dot(
            out_grad.astype(jnp.bfloat16),
            every[q].reshape(plane, depth),
            preferred_element_type=jnp.float32,
        )

    @pl.when(is_last)
    def _():
        @pl.loop(0, last)
        def _(q):
            slice_copy(q).wait_send()
            gain_copy(q).wait_send()

        @pl.loop(0, chunks)
        def _(c):
            weight_copy(w_ref, c, w_up, up).wait_send()
            if down_hops:
                weight_copy(w_ref, c, w_down, down).wait_send()

    @pl.when(jnp.logical_not(is_last))
    def _():
        @pl.when(p < up_hops - 1)
        def _():
            @pl.loop(0, chunks)
            def _(c):
                weight_copy(w7, c, w_up, up).wait_send()

        @pl.when(p > up_hops)
        def _():
            @pl.loop(0, chunks)
            def _(c):
                weight_copy(w7, c, w_down, down).wait_send()

    own_values.wait_send()
    cross_copy(0).wait_send()
    sums.wait_send()

    @pl.loop(1, n_chips)
    def _(k):
        values_copy(k).wait_send()
        forward_copy(k).wait_send()

    @pl.loop(1, n_dp)
    def _(k):
        token_copy(k).wait_send()
        cross_copy(k).wait_send()
        same_copy(k).wait_send()
        column_copy(k).wait_send()
        term_copy(k).wait_send()
        stat_copy(k).wait_send()

    @pl.loop(1, n_pipe)
    def _(k):
        line_copy(0, hz, h_send, h_recv, k).wait_send()
        line_copy(1, tz, z_send, z_recv, k).wait_send()
        delta_copy(k).wait_send()

    @pl.loop(0, n_pipe)
    def _(q):
        output_copy(q).wait_send()

    for copy in copies:
        copy.wait_send()
    for c in range(RING_CHUNKS):
        for s in range(up_hops):
            ring_copy(below(s), c, r_up, up).wait_send()
        for s in range(down_hops):
            ring_copy(above(s), c, r_down, down).wait_send()


def sections(weight, values, gain, embed, section_input, final_gain, target, rest, ids, column, n_pipe, n_dp):
    dma = pltpu.SemaphoreType.DMA
    vmem = pltpu.VMEM
    half, full = jnp.bfloat16, jnp.float32
    width, depth = weight.shape
    tokens = values.shape[1]
    vrows, model = embed.shape
    per_pipe = n_dp // n_pipe
    step = model // BACK_CHUNKS
    plane = n_dp * tokens
    rows = vrows // n_dp
    cols = per_pipe * width
    chunks = width // W_CHUNK
    return pl.pallas_call(
        functools.partial(section_kernel, n_pipe, n_dp),
        out_shape=(
            jax.ShapeDtypeStruct((width, depth), full),
            jax.ShapeDtypeStruct((rows, cols), full),
        ),
        in_specs=[ANY] * 5 + [VMEM] * 5,
        out_specs=(VMEM, VMEM),
        scratch_shapes=[
            vmem((vrows, model), half),
            vmem((width, depth), half),
            vmem((width, depth), half),
            vmem((n_dp, tokens, depth), half),
            vmem((1, model), full),
            vmem((n_pipe, n_dp, tokens, depth), half),
            vmem((tokens, model), half),
            vmem((n_dp, tokens, width), half),
            vmem((2, n_dp, tokens, width), half),
            vmem((tokens, 128), full),
            vmem((tokens, 128), full),
            vmem((tokens, vrows), half),
            vmem((n_pipe, tokens, vrows), half),
            vmem((BACK_CHUNKS, tokens, step), half),
            vmem((BACK_CHUNKS, tokens, step), half),
            vmem((2, n_dp, tokens, width), half),
            vmem((n_pipe, per_pipe, tokens, width), half),
            vmem((n_pipe, per_pipe, tokens, width), half),
            vmem((n_dp, tokens, width), half),
            vmem((n_pipe, width, plane), half),
            vmem((n_pipe, width, plane), half),
            vmem((n_pipe, width, plane), half),
            vmem((n_dp, rows, cols), half),
            vmem((n_dp, rows, cols), half),
            vmem((2 * n_pipe, plane), full),
            vmem((n_dp, 2 * n_pipe, plane), full),
            vmem((2 * n_pipe, plane), full),
            dma((7,)), dma((chunks,)), dma((chunks,)), dma((chunks,)),
            dma, dma((n_pipe,)), dma, dma((n_pipe,)),
            dma((n_dp,)), dma((n_dp,)), dma((n_dp,)), dma((n_dp // 2,)), dma((n_dp // 2,)),
            dma((2, n_dp)), dma((2, n_dp)), dma((2,)), dma((BACK_CHUNKS,)), dma((BACK_CHUNKS,)),
            dma((n_pipe,)), dma((n_pipe,)), dma((n_pipe,)), dma((n_pipe,)), dma((n_pipe,)), dma((n_pipe,)),
            dma((n_dp,)), dma((n_dp,)),
            dma((n_pipe, RING_CHUNKS)), dma((n_pipe, RING_CHUNKS)), dma((n_pipe, RING_CHUNKS)),
            dma((n_pipe,)), dma((n_pipe,)), dma((n_dp,)), dma((n_dp,)), dma((n_dp,)), dma((n_dp,)),
        ],
        compiler_params=pltpu.CompilerParams(
            collective_id=0, has_side_effects=True, vmem_limit_bytes=56 * 1024 * 1024
        ),
        name="sections",
    )(weight, values, gain, embed, section_input, final_gain, target, rest, ids, column)


def per_device(
    section_proj,
    attn_values,
    post_gain,
    section_input,
    final_gain,
    embed_block,
    token_ids,
    target_ids,
    block_offset,
    rest_lse,
):
    n_pipe, n_dp = lax.axis_size("pipe"), lax.axis_size("dp")
    weight = section_proj[0]
    width, depth = weight.shape
    model = section_input.shape[2]
    vrows = embed_block.shape[0]
    count = section_input.shape[0] * section_input.shape[1]
    first_row = block_offset[0] + lax.axis_index("tensor") * vrows
    column = lax.dynamic_slice(post_gain, (0, lax.axis_index("dp") * width), (1, width))
    own_grad, tied = sections(
        weight,
        attn_values.reshape(n_pipe, count // n_pipe, depth),
        post_gain,
        embed_block,
        section_input.reshape(count, model),
        final_gain.reshape(1, model),
        target_ids.reshape(count, 1) - block_offset[0],
        rest_lse.reshape(count, 1),
        token_ids.reshape(1, count) - first_row,
        column.reshape(width, 1),
        n_pipe,
        n_dp,
    )
    return (own_grad[None], tied)


def solution(mesh):
    in_specs = (
        P("pipe", "dp", "tensor"),
        P("pipe", None, "dp", "tensor"),
        P("pipe", None),
        P(None, "dp", None),
        P(),
        P("tensor", None),
        P(None, "dp"),
        P(None, "dp"),
        P(),
        P(None, "dp"),
    )
    out_specs = (P("pipe", "dp", "tensor"), P(("tensor", "dp"), "pipe"))
    return jax.shard_map(
        per_device, mesh=mesh, in_specs=in_specs, out_specs=out_specs, check_vma=False
    )
```

time: 617 us -> 134 us (0.22)
  waiting for transfers between devices: 532 us -> 0 us
  Pallas kernels: 0 us -> 122 us
  matrix products: 46.3 us -> 0 us
  between operations: 14.9 us -> 1.3 us
  other arithmetic: 11.1 us -> 1.37 us
    reduce_scatter x2 -> x0, waiting for transfers between devices: 225 us -> none  [the longest x1 116 us: per_device(): lax.psum_scatter(lax.dot_general(out_grad, values, contract_first, prefer...]
    psum x3 -> x0, waiting for transfers between devices: 182 us -> none  [the longest x1 73.6 us: broadcast(): return lax.psum(block, axis)]
    pallas_call x0 -> x1, Pallas kernels: none -> 122 us  [sections(): pl.pallas_call(functools.partial(section_kernel, n_pipe, n_dp), out_shape...]
    all_gather x1 -> x0, waiting for transfers between devices: 89.5 us -> none  [per_device(): lax.all_gather(weight, 'dp', axis=0, tiled=True)]
    dot_general x6 -> x0, matrix products: 46.3 us -> none  [the longest x1 10.5 us: per_device(): lax.dot_general(delta, head_in, contract_first, preferred_element_type=jn...]
    unnamed x8 -> x0, waiting for transfers between devices: 35.8 us -> none
    reduce_sum x4 -> x0, other arithmetic: 6.38 us -> none  [the longest x2 3.9 us: normalize(): scale = lax.rsqrt(jnp.mean(value * value, axis=-1, keepdims=True) + EPS)]
  transfers between devices with their start and end apart: 7 -> 0, of which waited for: 7 -> 0; matrix products, arithmetic and copies ran while one was open for 2% -> 0% of each run, Pallas kernels for 0% -> 0%
where the time goes in v2:
time: 134 us
  Pallas kernels  122 us (91%)
  local copies, waits for them, and re-layouts  8.78 us (7%)
  other arithmetic  1.37 us (1%)
    pallas_call x1, Pallas kernels, sections(): pl.pallas_call(functools.partial(section_kernel, n_pipe, n_dp), out_shape...  122 us
    unnamed x4, local copies, waits for them, and re-layouts  3.12 us

profile of v2, /device:TPU:1, one launch (start us, length us, event | category | flops | bytes accessed | tf_op | source)
XLA Modules:
  0.0 133.7 jit_solution(7656721786449652517)
XLA Ops:
  1.3 0.8 dynamic-slice_bitcast_fusion
  2.0 0.7 broadcast_subtract_fusion
  2.7 0.6 sub.21.ids_ref
  3.3 0.7 broadcast_subtract_fusion.1
  4.0 1.3 %reshape.51.fgain_ref = f32[1,4608]{1,0:T(1,128)} reshape(f32[4608]{0:T(1024)} %param.14) | data formatting | bytes 36864 | tf_op jit(solution)/shard_map/reshape | solution.py:655
  5.4 0.7 sub.22.target_ref
  6.1 1.4 %reshape.54.rest_ref = f32[128,1]{1,0:T(8,128)} reshape(f32[4,32]{1,0:T(4,128)} %param.19) | data formatting | bytes 1024 | tf_op jit(solution)/shard_map/reshape | solution.py:657
  7.5 0.8 copy.16.column_ref
  8.3 122.3 %sections.1 = (f32[288,1024]{1,0:T(8,128)}, f32[64,576]{1,0:T(8,128)}) custom-call(bf16[288,1024]{1,0:T(8,128)(2,1)} %bitcast.11, bf16[8,16,1024]{2,1,0:T(8,128)(2,1)} %bitcast.12, f32[1,4608]{1,0:T(1,128)} %gain_ref.1, bf16[1024,4608]{1,0:T(8,128)(2,1)} %embed_ref.1, bf16[128,4608]{1,0:T(8,128)(2,1)} %bitcast.10, f32[1,4608]{1,0:T(1,128)} %reshape.51.fgain_ref, ...), custom_call_target="tpu_custom_call" | custom-call | tf_op jit(solution)/shard_map/sections/pallas_call | solution.py:577
  130.6 0.0 copy-start
  130.6 2.4 %copy.20 = f32[1,288,1024]{2,1,0:T(8,128)} copy(f32[1,288,1024]{2,1,0:T(8,128)} %bitcast.9) | data formatting | bytes 2359296
  133.1 0.0 copy-done
  133.1 0.7 copy.21
Async XLA Ops:
  130.6 2.5 %copy-start = (f32[64,576]{1,0:T(8,128)S(1)}, f32[64,576]{1,0:T(8,128)}, u32[]{:S(2)}) copy-start(f32[64,576]{1,0:T(8,128)} %get-tuple-element.9) | copy-start | bytes 442372

commit v3 on v2

--- a/solution.py
+++ b/solution.py
@@ -13,6 +13,7 @@
 MESH = pl.DeviceIdType.MESH
 ANY = pl.BlockSpec(memory_space=pl.ANY)
 VMEM = pl.BlockSpec(memory_space=pltpu.VMEM)
+SMEM = pl.BlockSpec(memory_space=pltpu.SMEM)
 CONTRACT_LAST = (((1,), (1,)), ((), ()))
 W_CHUNK = 32
 BACK_CHUNKS = 4
@@ -59,16 +60,27 @@
     return scale, value * scale
 
 
+def own_tokens(ref, first, tokens):
+    micro, per = ref.shape
+    lane = lax.broadcasted_iota(jnp.int32, (tokens, per), 1)
+    token = lax.broadcasted_iota(jnp.int32, (tokens, per), 0) + first
+    found = jnp.zeros((tokens, per), jnp.float32)
+    for m in range(micro):
+        row = jnp.broadcast_to(ref[m:m + 1, :].astype(jnp.float32), (tokens, per))
+        found = found + jnp.where(lane + m * per == token, row, 0.0)
+    return jnp.sum(found, axis=1, keepdims=True)
+
+
 def flatten(blocks):
     return jnp.concatenate(blocks, axis=1)
 
 
 def section_kernel(
     n_pipe, n_dp,
-    w_ref, a_ref, gain_ref, embed_ref, input_ref, fgain_ref, target_ref, rest_ref, ids_ref, column_ref,
+    w_ref, a_ref, gain_ref, embed_ref, input_ref, fgain_ref, target_ref, rest_ref, ids_ref, offset_ref,
     proj_ref, tied_ref,
     embed, w, w7, a7, g7, every, rows_in, part, parts, sum_out, sum_in, delta_out, delta_all,
-    back_out, back_in, block, hz, tz, col, tg, ps, ps_in, term, terms, stat, stats, coef,
+    back_out, back_in, block, hz, tz, col, tg, ps, ps_in, term, terms, stat, stats, coef, gains, column,
     l_sem, w_recv, w_up, w_down, s_recv, s_send, g_recv, g_send, a_recv, a_send, v_recv, v_send, v_fwd,
     p_recv, p_send, sum_sem, back_recv, back_send, d_recv, d_send, h_recv, h_send, z_recv, z_send,
     c_recv, c_send, r_recv, r_up, r_down, o_recv, o_send, t_recv, t_send, st_recv, st_send,
@@ -104,8 +116,10 @@
     load_weight = pltpu.make_async_copy(w_ref, w, l_sem.at[1])
     load_rows = pltpu.make_async_copy(input_ref.at[mine], rows_in, l_sem.at[2])
     load_values = pltpu.make_async_copy(a_ref, every.at[:, j], l_sem.at[3])
+    load_gains = pltpu.make_async_copy(gain_ref, gains, l_sem.at[7])
     load_weight.start()
     load_rows.start()
+    load_gains.start()
 
     barrier = pltpu.get_barrier_semaphore()
     greet_pipe(barrier, n_pipe)
@@ -128,6 +142,25 @@
 
     def weight_copy(source, c, sems, device):
         return remote(piece(source, c), piece(w7, c), sems.at[c], w_recv.at[c], device)
+
+    def values_copy(k):
+        q = lax.rem(chip + k, n_chips) * 2 + core
+        return remote(a_ref, every.at[:, j], v_send.at[k], v_recv.at[j], (p, t, q))
+
+    def behind(k):
+        return lax.rem(chip + n_chips - k, n_chips) * 2
+
+    def forward_copy(k):
+        owner = behind(k) + core
+        return remote(
+            every.at[:, owner], every.at[:, owner], v_fwd.at[k], v_recv.at[owner], (p, t, sibling)
+        )
+
+    def values_arrived(owner):
+        return remote(a_ref, every.at[:, owner], v_send.at[0], v_recv.at[owner], (p, t, sibling))
+
+    def sibling_copy():
+        return remote(a_ref, every.at[:, j], v_send.at[0], v_recv.at[j], (p, t, sibling))
 
     own_slice = pltpu.make_async_copy(a_ref.at[last], a7.at[j], l_sem.at[4])
     own_weight = pltpu.make_async_copy(w_ref, w7, l_sem.at[5])
@@ -154,26 +187,20 @@
         own_weight.start()
         own_gain.start()
 
+    @pl.loop(1, n_chips)
+    def _(k):
+        values_copy(k).start()
+
+    sibling_copy().start()
     load_values.start()
     load_embed.start()
 
-    def values_copy(k):
-        q = lax.rem(chip + k, n_chips) * 2 + core
-        return remote(a_ref, every.at[:, j], v_send.at[k], v_recv.at[j], (p, t, q))
-
-    def behind(k):
-        return lax.rem(chip + n_chips - k, n_chips) * 2
-
-    def forward_copy(k):
-        owner = behind(k) + core
-        return remote(
-            every.at[:, owner], every.at[:, owner], v_fwd.at[k], v_recv.at[owner], (p, t, sibling)
-        )
-
-    def values_arrived(owner):
-        return remote(a_ref, every.at[:, owner], v_send.at[0], v_recv.at[owner], (p, t, sibling))
-
-    own_values = remote(a_ref, every.at[:, j], v_send.at[0], v_recv.at[j], (p, t, sibling))
+    load_gains.wait()
+    wide = pl.cdiv(width, 128) * 128
+    turned = pltpu.roll(
+        jnp.broadcast_to(gains[...], (8, model)), lax.rem(model - width * j, model), 1
+    )
+    column[...] = turned[:, :wide].T[:width, 0:1]
 
     @pl.when(is_last)
     def _():
@@ -192,12 +219,6 @@
     @pl.loop(1, n_dp)
     def _(k):
         token_copy(k).start()
-
-    own_values.start()
-
-    @pl.loop(1, n_chips)
-    def _(k):
-        values_copy(k).start()
 
     @pl.when(is_last)
     def _():
@@ -258,80 +279,6 @@
         values_arrived(behind(k) + core).wait_recv()
         forward_copy(k).start()
 
-    load_rows.wait()
-    load_embed.wait()
-
-    @pl.loop(0, n_dp)
-    def _(k):
-        part_arrived(other, k).wait_recv()
-
-    @pl.loop(1, n_dp)
-    def _(k):
-        part_arrived(t, dp_at(k)).wait_recv()
-
-    output = flatten(
-        [parts[0, q].astype(jnp.float32) + parts[1, q].astype(jnp.float32) for q in range(n_dp)]
-    )
-    _, normed = normalize(output)
-    resid = rows_in[...].astype(jnp.float32) + normed * g7[...]
-    y_scale, y_normed = normalize(resid)
-    head_in = (y_normed * fgain_ref[...]).astype(jnp.bfloat16)
-    for b in range(n_dp):
-        block[0, b] = head_in[:, b * width:(b + 1) * width]
-
-    def line_copy(slot, dst, send, recv, k):
-        q = pipe_at(k)
-        return remote(
-            block.at[slot, pl.ds(q * per_pipe, per_pipe)], dst.at[p], send.at[k], recv.at[p], (q, t, j)
-        )
-
-    def line_arrived(slot, dst, send, recv, q):
-        return remote(block.at[slot, pl.ds(0, per_pipe)], dst.at[q], send.at[0], recv.at[q], (q, t, j))
-
-    @pl.loop(1, n_pipe)
-    def _(k):
-        line_copy(0, hz, h_send, h_recv, k).start()
-
-    for b in range(per_pipe):
-        hz[p, b] = block[0, p * per_pipe + b]
-
-    raw = lax.dot_general(head_in, embed[...], CONTRACT_LAST, preferred_element_type=jnp.float32)
-    capped = jnp.tanh(raw / CAP)
-    logits = CAP * capped
-    own_sum = jnp.sum(jnp.exp(logits), axis=1, keepdims=True)
-    sum_out[...] = jnp.broadcast_to(own_sum, sum_out.shape)
-    sums = remote(sum_out, sum_in, sum_sem.at[0], sum_sem.at[1], pair)
-    sums.start()
-    lane = lax.broadcasted_iota(jnp.int32, (tokens, vrows), 1)
-    hit = (target_ref[mine, :] - t * vrows == lane).astype(jnp.float32)
-    slope = 1.0 - capped * capped
-    sums.wait_recv()
-    log_total = jnp.log(own_sum + sum_in[:, 0:1])
-    rest = rest_ref[mine, :]
-    lse = jnp.maximum(rest, log_total) + jnp.log(1.0 + jnp.exp(-jnp.abs(rest - log_total)))
-    delta = ((jnp.exp(logits - lse) - hit) * slope).astype(jnp.bfloat16)
-    delta_out[...] = delta
-    delta_all[p] = delta
-
-    step = model // BACK_CHUNKS
-    copies = []
-    for c in range(BACK_CHUNKS):
-        grad = jnp.dot(delta, embed[:, c * step:(c + 1) * step], preferred_element_type=jnp.float32)
-        back_out[c] = grad.astype(jnp.bfloat16)
-        copy = remote(back_out.at[c], back_in.at[c], back_send.at[c], back_recv.at[c], pair)
-        copy.start()
-        copies.append(copy)
-
-    def delta_copy(k):
-        return remote(delta_out, delta_all.at[p], d_send.at[k], d_recv.at[p], (pipe_at(k), t, j))
-
-    def delta_arrived(q):
-        return remote(delta_out, delta_all.at[q], d_send.at[0], d_recv.at[q], (q, t, j))
-
-    @pl.loop(1, n_pipe)
-    def _(k):
-        delta_copy(k).start()
-
     load_weight.wait()
     load_values.wait()
     values_arrived(sibling).wait_recv()
@@ -350,11 +297,92 @@
         ).astype(jnp.bfloat16)
         output_copy(q).start()
 
+    load_rows.wait()
+    load_embed.wait()
+
+    @pl.loop(0, n_dp)
+    def _(k):
+        part_arrived(other, k).wait_recv()
+
+    @pl.loop(1, n_dp)
+    def _(k):
+        part_arrived(t, dp_at(k)).wait_recv()
+
+    output = flatten(
+        [parts[0, q].astype(jnp.float32) + parts[1, q].astype(jnp.float32) for q in range(n_dp)]
+    )
+    _, normed = normalize(output)
+    final_gain = fgain_ref[...].reshape(1, model)
+    resid = rows_in[...].astype(jnp.float32) + normed * g7[...]
+    y_scale, y_normed = normalize(resid)
+    head_in = (y_normed * final_gain).astype(jnp.bfloat16)
+    for b in range(n_dp):
+        block[0, b] = head_in[:, b * width:(b + 1) * width]
+
+    def line_copy(slot, dst, send, recv, k):
+        q = pipe_at(k)
+        return remote(
+            block.at[slot, pl.ds(q * per_pipe, per_pipe)], dst.at[p], send.at[k], recv.at[p], (q, t, j)
+        )
+
+    def line_arrived(slot, dst, send, recv, q):
+        return remote(block.at[slot, pl.ds(0, per_pipe)], dst.at[q], send.at[0], recv.at[q], (q, t, j))
+
+    @pl.loop(1, n_pipe)
+    def _(k):
+        line_copy(0, hz, h_send, h_recv, k).start()
+
+    for b in range(per_pipe):
+        hz[p, b] = block[0, p * per_pipe + b]
+
+    raw = lax.dot_general(head_in, embed[...], CONTRACT_LAST, preferred_element_type=jnp.float32)
+    capped = jnp.tanh(raw / CAP)
+    logits = CAP * capped
+    own_sum = jnp.sum(jnp.exp(logits), axis=1, keepdims=True)
+    sum_out[...] = jnp.broadcast_to(own_sum, sum_out.shape)
+
+    def sum_copy():
+        return remote(sum_out, sum_in, sum_sem.at[0], sum_sem.at[1], pair)
+
+    sum_copy().start()
+    lane = lax.broadcasted_iota(jnp.int32, (tokens, vrows), 1)
+    first_row = offset_ref[0] + t * vrows
+    target = own_tokens(target_ref, p * tokens, tokens)
+    hit = (target == (first_row + lane).astype(jnp.float32)).astype(jnp.float32)
+    slope = 1.0 - capped * capped
+    sum_copy().wait_recv()
+    log_total = jnp.log(own_sum + sum_in[:, 0:1])
+    rest = own_tokens(rest_ref, p * tokens, tokens)
+    lse = jnp.maximum(rest, log_total) + jnp.log(1.0 + jnp.exp(-jnp.abs(rest - log_total)))
+    delta = ((jnp.exp(logits - lse) - hit) * slope).astype(jnp.bfloat16)
+    delta_out[...] = delta
+    delta_all[p] = delta
+
+    step = model // BACK_CHUNKS
+
+    def back_copy(c):
+        return remote(back_out.at[c], back_in.at[c], back_send.at[c], back_recv.at[c], pair)
+
+    for c in range(BACK_CHUNKS):
+        grad = jnp.dot(delta, embed[:, c * step:(c + 1) * step], preferred_element_type=jnp.float32)
+        back_out[c] = grad.astype(jnp.bfloat16)
+        back_copy(c).start()
+
+    def delta_copy(k):
+        return remote(delta_out, delta_all.at[p], d_send.at[k], d_recv.at[p], (pipe_at(k), t, j))
+
+    def delta_arrived(q):
+        return remote(delta_out, delta_all.at[q], d_send.at[0], d_recv.at[q], (q, t, j))
+
+    @pl.loop(1, n_pipe)
+    def _(k):
+        delta_copy(k).start()
+
     grads = []
     for c in range(BACK_CHUNKS):
-        copies[c].wait_recv()
+        back_copy(c).wait_recv()
         grads.append(back_out[c].astype(jnp.float32) + back_in[c].astype(jnp.float32))
-    grad = flatten(grads) * fgain_ref[...]
+    grad = flatten(grads) * final_gain
     top = y_scale * (grad - y_normed * jnp.mean(grad * y_normed, axis=-1, keepdims=True))
     top = top.astype(jnp.bfloat16)
     for b in range(n_dp):
@@ -414,7 +442,8 @@
     top_cols = flatten([tz[:, b].reshape(count, width) for b in range(per_pipe)])
     delta_rows = delta_all[...].reshape(count, vrows).T
     row = lax.broadcasted_iota(jnp.int32, (vrows, count), 0)
-    used = (ids_ref[...] == row).astype(jnp.bfloat16)
+    ids = flatten([ids_ref[m:m + 1, :] for m in range(ids_ref.shape[0])])
+    used = (ids == first_row + row).astype(jnp.bfloat16)
     term[...] = (
         (
             jnp.dot(delta_rows, head_cols, preferred_element_type=jnp.float32)
@@ -451,7 +480,7 @@
     def _(q):
         output_copy(q).wait_recv()
         out = ps[q].astype(jnp.float32) + ps_in[q].astype(jnp.float32)
-        grad = tg[q].astype(jnp.float32) * column_ref[...]
+        grad = tg[q].astype(jnp.float32) * column[...]
         stat[pl.ds(q, 1), :] = jnp.sum(out * out, axis=0, keepdims=True)
         stat[pl.ds(n_pipe + q, 1), :] = jnp.sum(out * grad, axis=0, keepdims=True)
 
@@ -489,7 +518,7 @@
     @pl.loop(0, n_pipe)
     def _(q):
         out = ps[q].astype(jnp.float32) + ps_in[q].astype(jnp.float32)
-        grad = tg[q].astype(jnp.float32) * column_ref[...]
+        grad = tg[q].astype(jnp.float32) * column[...]
         out_grad = coef[pl.ds(q, 1), :] * (grad - out * coef[pl.ds(n_pipe + q, 1), :])
         proj_ref[...] += jnp.dot(
             out_grad.astype(jnp.bfloat16),
@@ -524,9 +553,9 @@
             def _(c):
                 weight_copy(w7, c, w_down, down).wait_send()
 
-    own_values.wait_send()
+    sibling_copy().wait_send()
     cross_copy(0).wait_send()
-    sums.wait_send()
+    sum_copy().wait_send()
 
     @pl.loop(1, n_chips)
     def _(k):
@@ -552,8 +581,8 @@
     def _(q):
         output_copy(q).wait_send()
 
-    for copy in copies:
-        copy.wait_send()
+    for c in range(BACK_CHUNKS):
+        back_copy(c).wait_send()
     for c in range(RING_CHUNKS):
         for s in range(up_hops):
             ring_copy(below(s), c, r_up, up).wait_send()
@@ -561,7 +590,7 @@
             ring_copy(above(s), c, r_down, down).wait_send()
 
 
-def sections(weight, values, gain, embed, section_input, final_gain, target, rest, ids, column, n_pipe, n_dp):
+def sections(weight, values, gain, embed, section_input, final_gain, target, rest, ids, offset, n_pipe, n_dp):
     dma = pltpu.SemaphoreType.DMA
     vmem = pltpu.VMEM
     half, full = jnp.bfloat16, jnp.float32
@@ -580,7 +609,7 @@
             jax.ShapeDtypeStruct((width, depth), full),
             jax.ShapeDtypeStruct((rows, cols), full),
         ),
-        in_specs=[ANY] * 5 + [VMEM] * 5,
+        in_specs=[ANY] * 5 + [VMEM] * 4 + [SMEM],
         out_specs=(VMEM, VMEM),
         scratch_shapes=[
             vmem((vrows, model), half),
@@ -610,7 +639,9 @@
             vmem((2 * n_pipe, plane), full),
             vmem((n_dp, 2 * n_pipe, plane), full),
             vmem((2 * n_pipe, plane), full),
-            dma((7,)), dma((chunks,)), dma((chunks,)), dma((chunks,)),
+            vmem((1, model), full),
+            vmem((width, 1), full),
+            dma((8,)), dma((chunks,)), dma((chunks,)), dma((chunks,)),
             dma, dma((n_pipe,)), dma, dma((n_pipe,)),
             dma((n_dp,)), dma((n_dp,)), dma((n_dp,)), dma((n_dp // 2,)), dma((n_dp // 2,)),
             dma((2, n_dp)), dma((2, n_dp)), dma((2,)), dma((BACK_CHUNKS,)), dma((BACK_CHUNKS,)),
@@ -623,7 +654,7 @@
             collective_id=0, has_side_effects=True, vmem_limit_bytes=56 * 1024 * 1024
         ),
         name="sections",
-    )(weight, values, gain, embed, section_input, final_gain, target, rest, ids, column)
+    )(weight, values, gain, embed, section_input, final_gain, target, rest, ids, offset)
 
 
 def per_device(
@@ -640,23 +671,18 @@
 ):
     n_pipe, n_dp = lax.axis_size("pipe"), lax.axis_size("dp")
     weight = section_proj[0]
-    width, depth = weight.shape
-    model = section_input.shape[2]
-    vrows = embed_block.shape[0]
     count = section_input.shape[0] * section_input.shape[1]
-    first_row = block_offset[0] + lax.axis_index("tensor") * vrows
-    column = lax.dynamic_slice(post_gain, (0, lax.axis_index("dp") * width), (1, width))
     own_grad, tied = sections(
         weight,
-        attn_values.reshape(n_pipe, count // n_pipe, depth),
+        attn_values.reshape(n_pipe, count // n_pipe, weight.shape[1]),
         post_gain,
         embed_block,
-        section_input.reshape(count, model),
-        final_gain.reshape(1, model),
-        target_ids.reshape(count, 1) - block_offset[0],
-        rest_lse.reshape(count, 1),
-        token_ids.reshape(1, count) - first_row,
-        column.reshape(width, 1),
+        section_input.reshape(count, section_input.shape[2]),
+        final_gain,
+        target_ids,
+        rest_lse,
+        token_ids,
+        block_offset,
         n_pipe,
         n_dp,
     )

time: 134 us -> 125 us (0.933)
  local copies, waits for them, and re-layouts: 8.78 us -> 3.12 us
  other arithmetic: 1.37 us -> 0 us
    reshape x4 -> x0, local copies, waits for them, and re-layouts: 4.31 us -> none  [the longest x2 1.57 us: per_device(): column.reshape(width, 1)]
    pallas_call x1, Pallas kernels: 122 us -> 121 us  [sections(): pl.pallas_call(functools.partial(section_kernel, n_pipe, n_dp), out_shape...]
    sub x2 -> x0, other arithmetic: 1.37 us -> none  [the longest x1 0.69 us: per_device(): token_ids.reshape(1, count) - first_row]
    sub x2 -> x0, local copies, waits for them, and re-layouts: 1.35 us -> none  [the longest x1 0.73 us: per_device(): target_ids.reshape(count, 1) - block_offset[0]]
where the time goes in v3:
time: 125 us
  Pallas kernels  121 us (97%)
  local copies, waits for them, and re-layouts  3.12 us (2%)
  between operations  1.3 us (1%)
    pallas_call x1, Pallas kernels, sections(): pl.pallas_call(functools.partial(section_kernel, n_pipe, n_dp), out_shape...  121 us
    unnamed x4, local copies, waits for them, and re-layouts  3.12 us

profile of v3, /device:TPU:1, one launch (start us, length us, event | category | flops | bytes accessed | tf_op | source)
XLA Modules:
  0.0 125.1 jit_solution(3803702420278563674)
XLA Ops:
  1.3 120.7 %sections.1 = (f32[288,1024]{1,0:T(8,128)}, f32[64,576]{1,0:T(8,128)}) custom-call(bf16[288,1024]{1,0:T(8,128)(2,1)} %bitcast.6, bf16[8,16,1024]{2,1,0:T(8,128)(2,1)} %bitcast.7, f32[1,4608]{1,0:T(1,128)} %gain_ref.1, bf16[1024,4608]{1,0:T(8,128)(2,1)} %embed_ref.1, bf16[128,4608]{1,0:T(8,128)(2,1)} %bitcast.4, f32[4608]{0:T(1024)} %fgain_ref.1, ...), custom_call_target="tpu_custom_call" | custom-call | tf_op jit(solution)/shard_map/sections/pallas_call | solution.py:606
  122.0 0.0 copy-start
  122.0 2.4 %copy.15 = f32[1,288,1024]{2,1,0:T(8,128)} copy(f32[1,288,1024]{2,1,0:T(8,128)} %bitcast.5) | data formatting | bytes 2359296
  124.5 0.0 copy-done
  124.5 0.7 copy.16
Async XLA Ops:
  122.0 2.5 %copy-start = (f32[64,576]{1,0:T(8,128)S(1)}, f32[64,576]{1,0:T(8,128)}, u32[]{:S(2)}) copy-start(f32[64,576]{1,0:T(8,128)} %get-tuple-element.9) | copy-start | bytes 442372

commit v4 on v3

--- a/solution.py
+++ b/solution.py
@@ -81,7 +81,7 @@
     proj_ref, tied_ref,
     embed, w, w7, a7, g7, every, rows_in, part, parts, sum_out, sum_in, delta_out, delta_all,
     back_out, back_in, block, hz, tz, col, tg, ps, ps_in, term, terms, stat, stats, coef, gains, column,
-    l_sem, w_recv, w_up, w_down, s_recv, s_send, g_recv, g_send, a_recv, a_send, v_recv, v_send, v_fwd,
+    l_sem, w_recv, w_up, w_down, s_recv, s_send, g_recv, g_send, a_recv, a_send, a_fwd, v_recv, v_send, v_relay, v_fwd,
     p_recv, p_send, sum_sem, back_recv, back_send, d_recv, d_send, h_recv, h_send, z_recv, z_send,
     c_recv, c_send, r_recv, r_up, r_down, o_recv, o_send, t_recv, t_send, st_recv, st_send,
 ):
@@ -93,7 +93,11 @@
     core = lax.rem(j, 2)
     sibling = j + 1 - 2 * core
     n_chips = n_dp // 2
+    n_rows = n_chips // 2
     chip = j // 2
+    side = lax.rem(chip, 2)
+    line = chip // 2
+    across = 2 * (chip + 1 - 2 * side) + core
     chunks = w_ref.shape[0] // W_CHUNK
     is_last = p == last
     up = (lax.rem(p + 1, n_pipe), t, j)
@@ -143,24 +147,27 @@
     def weight_copy(source, c, sems, device):
         return remote(piece(source, c), piece(w7, c), sems.at[c], w_recv.at[c], device)
 
-    def values_copy(k):
-        q = lax.rem(chip + k, n_chips) * 2 + core
-        return remote(a_ref, every.at[:, j], v_send.at[k], v_recv.at[j], (p, t, q))
-
-    def behind(k):
-        return lax.rem(chip + n_chips - k, n_chips) * 2
-
-    def forward_copy(k):
-        owner = behind(k) + core
-        return remote(
-            every.at[:, owner], every.at[:, owner], v_fwd.at[k], v_recv.at[owner], (p, t, sibling)
-        )
+    def along(k):
+        return (lax.rem(line + k, n_rows) * 2 + side) * 2 + core
+
+    def source_of(k, far):
+        place = lax.rem(line + n_rows - k, n_rows) * 2
+        return (place + (1 - side if far else side)) * 2 + core
+
+    def values_copy(q, sem):
+        return remote(a_ref, every.at[:, j], v_send.at[sem], v_recv.at[j], (p, t, q))
+
+    def pass_copy(owner, q, sem):
+        return remote(every.at[:, owner], every.at[:, owner], sem, v_recv.at[owner], (p, t, q))
+
+    def relay_copy(k):
+        return pass_copy(across, along(k), v_relay.at[k])
+
+    def forward_copy(k, far):
+        return pass_copy(source_of(k, far), sibling, v_fwd.at[k + (n_rows if far else 0)])
 
     def values_arrived(owner):
         return remote(a_ref, every.at[:, owner], v_send.at[0], v_recv.at[owner], (p, t, sibling))
-
-    def sibling_copy():
-        return remote(a_ref, every.at[:, j], v_send.at[0], v_recv.at[j], (p, t, sibling))
 
     own_slice = pltpu.make_async_copy(a_ref.at[last], a7.at[j], l_sem.at[4])
     own_weight = pltpu.make_async_copy(w_ref, w7, l_sem.at[5])
@@ -187,11 +194,13 @@
         own_weight.start()
         own_gain.start()
 
-    @pl.loop(1, n_chips)
-    def _(k):
-        values_copy(k).start()
-
-    sibling_copy().start()
+    values_copy(across, 1).start()
+
+    @pl.loop(1, n_rows)
+    def _(k):
+        values_copy(along(k), k + 1).start()
+
+    values_copy(sibling, 0).start()
     load_values.start()
     load_embed.start()
 
@@ -211,17 +220,42 @@
         slice_copy(p).wait_recv()
 
     def token_copy(k):
-        return remote(a7.at[j], a7.at[j], a_send.at[k], a_recv.at[j], (p, t, dp_at(k)))
+        q = lax.rem(chip + k, n_chips) * 2 + core
+        return remote(a7.at[j], a7.at[j], a_send.at[k], a_recv.at[j], (p, t, q))
 
     def tokens_arrived(q):
         return remote(a7.at[j], a7.at[q], a_send.at[0], a_recv.at[q], (p, t, sibling))
 
-    @pl.loop(1, n_dp)
+    def tokens_forward(k):
+        owner = lax.rem(chip + n_chips - k, n_chips) * 2 + core
+        return remote(a7.at[owner], a7.at[owner], a_fwd.at[k], a_recv.at[owner], (p, t, sibling))
+
+    @pl.loop(1, n_chips)
     def _(k):
         token_copy(k).start()
+
+    tokens_forward(0).start()
+
+    def relay():
+        values_arrived(across).wait_recv()
+
+        @pl.loop(1, n_rows)
+        def _(k):
+            relay_copy(k).start()
+
+        forward_copy(0, True).start()
+
+        @pl.loop(1, n_chips)
+        def _(k):
+            tokens_arrived(lax.rem(chip + n_chips - k, n_chips) * 2 + core).wait_recv()
+            tokens_forward(k).start()
+
+    next_to_last = jnp.logical_or(p == 0, p == last - 1)
+    relay_at = jnp.where(next_to_last, min(4, chunks - 1), 0)
 
     @pl.when(is_last)
     def _():
+        relay()
         own_weight.wait()
         own_gain.wait()
 
@@ -239,11 +273,15 @@
             def _():
                 weight_copy(w7, c, w_down, down).start()
 
+            @pl.when(c == relay_at)
+            def _():
+                relay()
+
         gain_copy(p).wait_recv()
 
-    @pl.loop(1, n_dp)
-    def _(k):
-        tokens_arrived(dp_at(k)).wait_recv()
+    @pl.loop(0, n_chips)
+    def _(k):
+        tokens_arrived(2 * k + 1 - core).wait_recv()
 
     part[...] = (
         lax.dot_general(
@@ -274,18 +312,18 @@
 
     parts[t, j] = part[j]
 
-    @pl.loop(1, n_chips)
-    def _(k):
-        values_arrived(behind(k) + core).wait_recv()
-        forward_copy(k).start()
+    @pl.loop(1, n_rows)
+    def _(k):
+        for far in (False, True):
+            values_arrived(source_of(k, far)).wait_recv()
+            forward_copy(k, far).start()
 
     load_weight.wait()
     load_values.wait()
-    values_arrived(sibling).wait_recv()
-
-    @pl.loop(1, n_chips)
-    def _(k):
-        values_arrived(behind(k) + 1 - core).wait_recv()
+
+    @pl.loop(0, n_chips)
+    def _(k):
+        values_arrived(2 * k + 1 - core).wait_recv()
 
     def output_copy(q):
         return remote(ps.at[q], ps_in.at[q], o_send.at[q], o_recv.at[q], pair)
@@ -553,18 +591,27 @@
             def _(c):
                 weight_copy(w7, c, w_down, down).wait_send()
 
-    sibling_copy().wait_send()
+    values_copy(sibling, 0).wait_send()
+    values_copy(across, 1).wait_send()
+    forward_copy(0, True).wait_send()
+    tokens_forward(0).wait_send()
     cross_copy(0).wait_send()
     sum_copy().wait_send()
 
+    @pl.loop(1, n_rows)
+    def _(k):
+        values_copy(along(k), k + 1).wait_send()
+        relay_copy(k).wait_send()
+        forward_copy(k, False).wait_send()
+        forward_copy(k, True).wait_send()
+
     @pl.loop(1, n_chips)
     def _(k):
-        values_copy(k).wait_send()
-        forward_copy(k).wait_send()
-
-    @pl.loop(1, n_dp)
-    def _(k):
         token_copy(k).wait_send()
+        tokens_forward(k).wait_send()
+
+    @pl.loop(1, n_dp)
+    def _(k):
         cross_copy(k).wait_send()
         same_copy(k).wait_send()
         column_copy(k).wait_send()
@@ -643,7 +690,8 @@
             vmem((width, 1), full),
             dma((8,)), dma((chunks,)), dma((chunks,)), dma((chunks,)),
             dma, dma((n_pipe,)), dma, dma((n_pipe,)),
-            dma((n_dp,)), dma((n_dp,)), dma((n_dp,)), dma((n_dp // 2,)), dma((n_dp // 2,)),
+            dma((n_dp,)), dma((n_dp // 2,)), dma((n_dp // 2,)),
+            dma((n_dp,)), dma((n_dp // 4 + 1,)), dma((n_dp // 4,)), dma((n_dp // 2,)),
             dma((2, n_dp)), dma((2, n_dp)), dma((2,)), dma((BACK_CHUNKS,)), dma((BACK_CHUNKS,)),
             dma((n_pipe,)), dma((n_pipe,)), dma((n_pipe,)), dma((n_pipe,)), dma((n_pipe,)), dma((n_pipe,)),
             dma((n_dp,)), dma((n_dp,)),

time: 125 us -> 121 us (0.968)
  Pallas kernels: 121 us -> 117 us
    pallas_call x1, Pallas kernels: 121 us -> 117 us  [sections(): pl.pallas_call(functools.partial(section_kernel, n_pipe, n_dp), out_shape...]
where the time goes in v4:
time: 121 us
  Pallas kernels  117 us (97%)
  local copies, waits for them, and re-layouts  3.12 us (3%)
  between operations  1.3 us (1%)
    pallas_call x1, Pallas kernels, sections(): pl.pallas_call(functools.partial(section_kernel, n_pipe, n_dp), out_shape...  117 us
    unnamed x4, local copies, waits for them, and re-layouts  3.12 us

profile of v4, /device:TPU:1, one launch (start us, length us, event | category | flops | bytes accessed | tf_op | source)
XLA Modules:
  0.0 121.0 jit_solution(1144957508197624060)
XLA Ops:
  1.3 116.6 %sections.1 = (f32[288,1024]{1,0:T(8,128)}, f32[64,576]{1,0:T(8,128)}) custom-call(bf16[288,1024]{1,0:T(8,128)(2,1)} %bitcast.6, bf16[8,16,1024]{2,1,0:T(8,128)(2,1)} %bitcast.7, f32[1,4608]{1,0:T(1,128)} %gain_ref.1, bf16[1024,4608]{1,0:T(8,128)(2,1)} %embed_ref.1, bf16[128,4608]{1,0:T(8,128)(2,1)} %bitcast.4, f32[4608]{0:T(1024)} %fgain_ref.1, ...), custom_call_target="tpu_custom_call" | custom-call | tf_op jit(solution)/shard_map/sections/pallas_call | solution.py:653
  117.9 0.0 copy-start
  117.9 2.4 %copy.15 = f32[1,288,1024]{2,1,0:T(8,128)} copy(f32[1,288,1024]{2,1,0:T(8,128)} %bitcast.5) | data formatting | bytes 2359296
  120.4 0.0 copy-done
  120.4 0.7 copy.16
Async XLA Ops:
  117.9 2.5 %copy-start = (f32[64,576]{1,0:T(8,128)S(1)}, f32[64,576]{1,0:T(8,128)}, u32[]{:S(2)}) copy-start(f32[64,576]{1,0:T(8,128)} %get-tuple-element.9) | copy-start | bytes 442372

commit v5 on v4

--- a/solution.py
+++ b/solution.py
@@ -80,10 +80,10 @@
     w_ref, a_ref, gain_ref, embed_ref, input_ref, fgain_ref, target_ref, rest_ref, ids_ref, offset_ref,
     proj_ref, tied_ref,
     embed, w, w7, a7, g7, every, rows_in, part, parts, sum_out, sum_in, delta_out, delta_all,
-    back_out, back_in, block, hz, tz, col, tg, ps, ps_in, term, terms, stat, stats, coef, gains, column,
+    back_out, back_in, block, hz, tz, col, tg, ps, ps_in, term, core_in, half, line_in, side_out, side_in, stat, stats, coef, gains, column,
     l_sem, w_recv, w_up, w_down, s_recv, s_send, g_recv, g_send, a_recv, a_send, a_fwd, v_recv, v_send, v_relay, v_fwd,
     p_recv, p_send, sum_sem, back_recv, back_send, d_recv, d_send, h_recv, h_send, z_recv, z_send,
-    c_recv, c_send, r_recv, r_up, r_down, o_recv, o_send, t_recv, t_send, st_recv, st_send,
+    c_recv, c_send, r_recv, r_up, r_down, o_recv, o_send, t_recv, t_send, y_recv, y_send, x_sem, st_recv, st_send,
 ):
     p, t, j = position()
     last = n_pipe - 1
@@ -333,7 +333,13 @@
         ps[q] = lax.dot_general(
             w[...], every[q].reshape(plane, depth), CONTRACT_LAST, preferred_element_type=jnp.float32
         ).astype(jnp.bfloat16)
-        output_copy(q).start()
+
+    def send_outputs(first, stop):
+        @pl.loop(first, stop)
+        def _(q):
+            output_copy(q).start()
+
+    send_outputs(0, n_pipe // 4)
 
     load_rows.wait()
     load_embed.wait()
@@ -346,6 +352,7 @@
     def _(k):
         part_arrived(t, dp_at(k)).wait_recv()
 
+    send_outputs(n_pipe // 4, n_pipe // 2)
     output = flatten(
         [parts[0, q].astype(jnp.float32) + parts[1, q].astype(jnp.float32) for q in range(n_dp)]
     )
@@ -467,6 +474,7 @@
         ring_copy(p, c, r_up, up).start()
         if down_hops:
             ring_copy(p, c, r_down, down).start()
+    send_outputs(n_pipe // 2, n_pipe)
 
     @pl.loop(1, n_pipe)
     def _(k):
@@ -491,18 +499,47 @@
         .reshape(term.shape)
     )
 
-    def term_copy(k):
-        q = dp_at(k)
-        return remote(term.at[q], terms.at[j], t_send.at[k], t_recv.at[j], (p, t, q))
-
-    def term_arrived(q):
-        return remote(term.at[q], terms.at[q], t_send.at[0], t_recv.at[q], pair)
-
-    @pl.loop(1, n_dp)
-    def _(k):
-        term_copy(k).start()
-
-    terms[j] = term[j]
+    def core_copy(k):
+        return remote(term.at[2 * k + 1 - core], core_in.at[k], t_send.at[k], t_recv.at[k], (p, t, sibling))
+
+    def line_term(k):
+        q = lax.rem(line + k, n_rows)
+        return remote(
+            half.at[pl.ds(2 * q, 2)], line_in.at[line], y_send.at[k], y_recv.at[line], (p, t, along(k))
+        )
+
+    def line_term_arrived(q):
+        return remote(half.at[pl.ds(0, 2)], line_in.at[q], y_send.at[0], y_recv.at[q], (p, t, sibling))
+
+    def side_copy():
+        return remote(side_out, side_in, x_sem.at[0], x_sem.at[1], (p, t, across))
+
+    def sum_cores():
+        @pl.loop(0, n_chips)
+        def _(k):
+            core_copy(k).wait_recv()
+            both = term[2 * k + core].astype(jnp.float32) + core_in[k].astype(jnp.float32)
+            half[k] = both.astype(jnp.bfloat16)
+
+        @pl.loop(1, n_rows)
+        def _(k):
+            line_term(k).start()
+
+    def sum_line():
+        near = half[2 * line + side].astype(jnp.float32)
+        far = half[2 * line + 1 - side].astype(jnp.float32)
+        for k in range(1, n_rows):
+            q = lax.rem(line + n_rows - k, n_rows)
+            line_term_arrived(q).wait_recv()
+            near = near + line_in[q, side].astype(jnp.float32)
+            far = far + line_in[q, 1 - side].astype(jnp.float32)
+        tied_ref[...] = near
+        side_out[...] = far.astype(jnp.bfloat16)
+        side_copy().start()
+
+    @pl.loop(0, n_chips)
+    def _(k):
+        core_copy(k).start()
 
     for s in range(1, up_hops + 1):
         for c in range(RING_CHUNKS):
@@ -513,6 +550,12 @@
                 ring_copy(above(s), c, r_down, down).wait_recv()
                 if s < down_hops:
                     ring_copy(above(s), c, r_down, down).start()
+        if s == 1:
+            sum_cores()
+        if s == up_hops - 1:
+            sum_line()
+    if up_hops == 1:
+        sum_line()
 
     @pl.loop(0, n_pipe)
     def _(q):
@@ -534,14 +577,8 @@
 
     stats[j] = stat[...]
 
-    @pl.loop(1, n_dp)
-    def _(k):
-        term_arrived(dp_at(k)).wait_recv()
-
-    total = terms[0].astype(jnp.float32)
-    for q in range(1, n_dp):
-        total = total + terms[q].astype(jnp.float32)
-    tied_ref[...] = total
+    side_copy().wait_recv()
+    tied_ref[...] += side_in[...].astype(jnp.float32)
 
     @pl.loop(1, n_dp)
     def _(k):
@@ -615,7 +652,6 @@
         cross_copy(k).wait_send()
         same_copy(k).wait_send()
         column_copy(k).wait_send()
-        term_copy(k).wait_send()
         stat_copy(k).wait_send()
 
     @pl.loop(1, n_pipe)
@@ -628,6 +664,15 @@
     def _(q):
         output_copy(q).wait_send()
 
+    @pl.loop(0, n_chips)
+    def _(k):
+        core_copy(k).wait_send()
+
+    @pl.loop(1, n_rows)
+    def _(k):
+        line_term(k).wait_send()
+
+    side_copy().wait_send()
     for c in range(BACK_CHUNKS):
         back_copy(c).wait_send()
     for c in range(RING_CHUNKS):
@@ -682,7 +727,11 @@
             vmem((n_pipe, width, plane), half),
             vmem((n_pipe, width, plane), half),
             vmem((n_dp, rows, cols), half),
-            vmem((n_dp, rows, cols), half),
+            vmem((n_dp // 2, rows, cols), half),
+            vmem((n_dp // 2, rows, cols), half),
+            vmem((n_dp // 4, 2, rows, cols), half),
+            vmem((rows, cols), half),
+            vmem((rows, cols), half),
             vmem((2 * n_pipe, plane), full),
             vmem((n_dp, 2 * n_pipe, plane), full),
             vmem((2 * n_pipe, plane), full),
@@ -696,7 +745,8 @@
             dma((n_pipe,)), dma((n_pipe,)), dma((n_pipe,)), dma((n_pipe,)), dma((n_pipe,)), dma((n_pipe,)),
             dma((n_dp,)), dma((n_dp,)),
             dma((n_pipe, RING_CHUNKS)), dma((n_pipe, RING_CHUNKS)), dma((n_pipe, RING_CHUNKS)),
-            dma((n_pipe,)), dma((n_pipe,)), dma((n_dp,)), dma((n_dp,)), dma((n_dp,)), dma((n_dp,)),
+            dma((n_pipe,)), dma((n_pipe,)), dma((n_dp // 2,)), dma((n_dp // 2,)),
+            dma((n_dp // 4,)), dma((n_dp // 4,)), dma((2,)), dma((n_dp,)), dma((n_dp,)),
         ],
         compiler_params=pltpu.CompilerParams(
             collective_id=0, has_side_effects=True, vmem_limit_bytes=56 * 1024 * 1024

time: 121 us -> 110 us (0.909)
  Pallas kernels: 117 us -> 106 us
    pallas_call x1, Pallas kernels: 117 us -> 106 us  [sections(): pl.pallas_call(functools.partial(section_kernel, n_pipe, n_dp), out_shape...]
where the time goes in v5:
time: 110 us
  Pallas kernels  106 us (96%)
  local copies, waits for them, and re-layouts  3.12 us (3%)
  between operations  1.3 us (1%)
    pallas_call x1, Pallas kernels, sections(): pl.pallas_call(functools.partial(section_kernel, n_pipe, n_dp), out_shape...  106 us
    unnamed x4, local copies, waits for them, and re-layouts  3.12 us

profile of v5, /device:TPU:1, one launch (start us, length us, event | category | flops | bytes accessed | tf_op | source)
XLA Modules:
  0.0 110.2 jit_solution(8816853443854557114)
XLA Ops:
  1.3 105.8 %sections.1 = (f32[288,1024]{1,0:T(8,128)}, f32[64,576]{1,0:T(8,128)}) custom-call(bf16[288,1024]{1,0:T(8,128)(2,1)} %bitcast.6, bf16[8,16,1024]{2,1,0:T(8,128)(2,1)} %bitcast.7, f32[1,4608]{1,0:T(1,128)} %gain_ref.1, bf16[1024,4608]{1,0:T(8,128)(2,1)} %embed_ref.1, bf16[128,4608]{1,0:T(8,128)(2,1)} %bitcast.4, f32[4608]{0:T(1024)} %fgain_ref.1, ...), custom_call_target="tpu_custom_call" | custom-call | tf_op jit(solution)/shard_map/sections/pallas_call | solution.py:698
  107.0 0.0 copy-start
  107.1 2.4 %copy.15 = f32[1,288,1024]{2,1,0:T(8,128)} copy(f32[1,288,1024]{2,1,0:T(8,128)} %bitcast.5) | data formatting | bytes 2359296
  109.5 0.0 copy-done
  109.5 0.7 copy.16
Async XLA Ops:
  107.0 2.5 %copy-start = (f32[64,576]{1,0:T(8,128)S(1)}, f32[64,576]{1,0:T(8,128)}, u32[]{:S(2)}) copy-start(f32[64,576]{1,0:T(8,128)} %get-tuple-element.9) | copy-start | bytes 442372

commit v6 on v5

--- a/solution.py
+++ b/solution.py
@@ -80,7 +80,7 @@
     w_ref, a_ref, gain_ref, embed_ref, input_ref, fgain_ref, target_ref, rest_ref, ids_ref, offset_ref,
     proj_ref, tied_ref,
     embed, w, w7, a7, g7, every, rows_in, part, parts, sum_out, sum_in, delta_out, delta_all,
-    back_out, back_in, block, hz, tz, col, tg, ps, ps_in, term, core_in, half, line_in, side_out, side_in, stat, stats, coef, gains, column,
+    back_out, back_in, block, line_out, hz, tz, col, tg, ps, ps_in, term, core_in, half, line_in, side_out, side_in, stat, stats, coef, gains, column,
     l_sem, w_recv, w_up, w_down, s_recv, s_send, g_recv, g_send, a_recv, a_send, a_fwd, v_recv, v_send, v_relay, v_fwd,
     p_recv, p_send, sum_sem, back_recv, back_send, d_recv, d_send, h_recv, h_send, z_recv, z_send,
     c_recv, c_send, r_recv, r_up, r_down, o_recv, o_send, t_recv, t_send, y_recv, y_send, x_sem, st_recv, st_send,
@@ -105,7 +105,6 @@
     pair = (p, other, j)
     tokens, width = part.shape[1:]
     vrows, model = embed.shape
-    per_pipe = n_dp // n_pipe
     plane = n_dp * tokens
     depth = w.shape[1]
     mine = pl.ds(pl.multiple_of(p * tokens, tokens), tokens)
@@ -339,6 +338,7 @@
         def _(q):
             output_copy(q).start()
 
+    after_parts = n_pipe // 2 - n_pipe // 8
     send_outputs(0, n_pipe // 4)
 
     load_rows.wait()
@@ -352,7 +352,7 @@
     def _(k):
         part_arrived(t, dp_at(k)).wait_recv()
 
-    send_outputs(n_pipe // 4, n_pipe // 2)
+    send_outputs(n_pipe // 4, after_parts)
     output = flatten(
         [parts[0, q].astype(jnp.float32) + parts[1, q].astype(jnp.float32) for q in range(n_dp)]
     )
@@ -361,24 +361,22 @@
     resid = rows_in[...].astype(jnp.float32) + normed * g7[...]
     y_scale, y_normed = normalize(resid)
     head_in = (y_normed * final_gain).astype(jnp.bfloat16)
-    for b in range(n_dp):
-        block[0, b] = head_in[:, b * width:(b + 1) * width]
+    cols = hz.shape[2]
+    for q in range(n_pipe):
+        line_out[0, q] = head_in[:, q * cols:(q + 1) * cols]
 
     def line_copy(slot, dst, send, recv, k):
         q = pipe_at(k)
-        return remote(
-            block.at[slot, pl.ds(q * per_pipe, per_pipe)], dst.at[p], send.at[k], recv.at[p], (q, t, j)
-        )
+        return remote(line_out.at[slot, q], dst.at[p], send.at[k], recv.at[p], (q, t, j))
 
     def line_arrived(slot, dst, send, recv, q):
-        return remote(block.at[slot, pl.ds(0, per_pipe)], dst.at[q], send.at[0], recv.at[q], (q, t, j))
+        return remote(line_out.at[slot, q], dst.at[q], send.at[0], recv.at[q], (q, t, j))
 
     @pl.loop(1, n_pipe)
     def _(k):
         line_copy(0, hz, h_send, h_recv, k).start()
 
-    for b in range(per_pipe):
-        hz[p, b] = block[0, p * per_pipe + b]
+    hz[p] = line_out[0, p]
 
     raw = lax.dot_general(head_in, embed[...], CONTRACT_LAST, preferred_element_type=jnp.float32)
     capped = jnp.tanh(raw / CAP)
@@ -431,14 +429,16 @@
     top = y_scale * (grad - y_normed * jnp.mean(grad * y_normed, axis=-1, keepdims=True))
     top = top.astype(jnp.bfloat16)
     for b in range(n_dp):
-        block[1, b] = top[:, b * width:(b + 1) * width]
+        block[b] = top[:, b * width:(b + 1) * width]
+    for q in range(n_pipe):
+        line_out[1, q] = top[:, q * cols:(q + 1) * cols]
 
     def column_copy(k):
         q = dp_at(k)
-        return remote(block.at[1, q], col.at[j], c_send.at[k], c_recv.at[j], (p, t, q))
+        return remote(block.at[q], col.at[j], c_send.at[k], c_recv.at[j], (p, t, q))
 
     def column_arrived(q):
-        return remote(block.at[1, q], col.at[q], c_send.at[0], c_recv.at[q], pair)
+        return remote(block.at[q], col.at[q], c_send.at[0], c_recv.at[q], pair)
 
     @pl.loop(1, n_dp)
     def _(k):
@@ -448,9 +448,9 @@
     def _(k):
         line_copy(1, tz, z_send, z_recv, k).start()
 
-    col[j] = block[1, j]
-    for b in range(per_pipe):
-        tz[p, b] = block[1, p * per_pipe + b]
+    send_outputs(after_parts, n_pipe // 2)
+    col[j] = block[j]
+    tz[p] = line_out[1, p]
 
     @pl.loop(1, n_dp)
     def _(k):
@@ -484,8 +484,8 @@
         delta_arrived(q).wait_recv()
 
     count = n_pipe * tokens
-    head_cols = flatten([hz[:, b].reshape(count, width) for b in range(per_pipe)])
-    top_cols = flatten([tz[:, b].reshape(count, width) for b in range(per_pipe)])
+    head_cols = hz[...].reshape(count, cols)
+    top_cols = tz[...].reshape(count, cols)
     delta_rows = delta_all[...].reshape(count, vrows).T
     row = lax.broadcasted_iota(jnp.int32, (vrows, count), 0)
     ids = flatten([ids_ref[m:m + 1, :] for m in range(ids_ref.shape[0])])
@@ -719,9 +719,10 @@
             vmem((n_pipe, tokens, vrows), half),
             vmem((BACK_CHUNKS, tokens, step), half),
             vmem((BACK_CHUNKS, tokens, step), half),
-            vmem((2, n_dp, tokens, width), half),
-            vmem((n_pipe, per_pipe, tokens, width), half),
-            vmem((n_pipe, per_pipe, tokens, width), half),
+            vmem((n_dp, tokens, width), half),
+            vmem((2, n_pipe, tokens, cols), half),
+            vmem((n_pipe, tokens, cols), half),
+            vmem((n_pipe, tokens, cols), half),
             vmem((n_dp, tokens, width), half),
             vmem((n_pipe, width, plane), half),
             vmem((n_pipe, width, plane), half),

time: 110 us -> 107 us (0.973)
  Pallas kernels: 106 us -> 102 us
    pallas_call x1, Pallas kernels: 106 us -> 102 us  [sections(): pl.pallas_call(functools.partial(section_kernel, n_pipe, n_dp), out_shape...]
where the time goes in v6:
time: 107 us
  Pallas kernels  102 us (95%)
  local copies, waits for them, and re-layouts  3.12 us (3%)
  between operations  1.3 us (1%)
    pallas_call x1, Pallas kernels, sections(): pl.pallas_call(functools.partial(section_kernel, n_pipe, n_dp), out_shape...  102 us
    unnamed x4, local copies, waits for them, and re-layouts  3.12 us

profile of v6, /device:TPU:1, one launch (start us, length us, event | category | flops | bytes accessed | tf_op | source)
XLA Modules:
  0.0 106.7 jit_solution(11809784814291508828)
XLA Ops:
  1.3 102.3 %sections.1 = (f32[288,1024]{1,0:T(8,128)}, f32[64,576]{1,0:T(8,128)}) custom-call(bf16[288,1024]{1,0:T(8,128)(2,1)} %bitcast.6, bf16[8,16,1024]{2,1,0:T(8,128)(2,1)} %bitcast.7, f32[1,4608]{1,0:T(1,128)} %gain_ref.1, bf16[1024,4608]{1,0:T(8,128)(2,1)} %embed_ref.1, bf16[128,4608]{1,0:T(8,128)(2,1)} %bitcast.4, f32[4608]{0:T(1024)} %fgain_ref.1, ...), custom_call_target="tpu_custom_call" | custom-call | tf_op jit(solution)/shard_map/sections/pallas_call | solution.py:698
  103.6 0.0 copy-start
  103.6 2.4 %copy.15 = f32[1,288,1024]{2,1,0:T(8,128)} copy(f32[1,288,1024]{2,1,0:T(8,128)} %bitcast.5) | data formatting | bytes 2359296
  106.0 0.0 copy-done
  106.0 0.7 copy.16
Async XLA Ops:
  103.6 2.5 %copy-start = (f32[64,576]{1,0:T(8,128)S(1)}, f32[64,576]{1,0:T(8,128)}, u32[]{:S(2)}) copy-start(f32[64,576]{1,0:T(8,128)} %get-tuple-element.9) | copy-start | bytes 442372

commit v7 on v6

--- a/solution.py
+++ b/solution.py
@@ -338,7 +338,6 @@
         def _(q):
             output_copy(q).start()
 
-    after_parts = n_pipe // 2 - n_pipe // 8
     send_outputs(0, n_pipe // 4)
 
     load_rows.wait()
@@ -352,7 +351,6 @@
     def _(k):
         part_arrived(t, dp_at(k)).wait_recv()
 
-    send_outputs(n_pipe // 4, after_parts)
     output = flatten(
         [parts[0, q].astype(jnp.float32) + parts[1, q].astype(jnp.float32) for q in range(n_dp)]
     )
@@ -448,7 +446,7 @@
     def _(k):
         line_copy(1, tz, z_send, z_recv, k).start()
 
-    send_outputs(after_parts, n_pipe // 2)
+    send_outputs(n_pipe // 4, n_pipe // 2)
     col[j] = block[j]
     tz[p] = line_out[1, p]
 

time: 107 us -> 104 us (0.972)
  Pallas kernels: 102 us -> 99.3 us
    pallas_call x1, Pallas kernels: 102 us -> 99.3 us  [sections(): pl.pallas_call(functools.partial(section_kernel, n_pipe, n_dp), out_shape...]
where the time goes in v7:
time: 104 us
  Pallas kernels  99.3 us (95%)
  local copies, waits for them, and re-layouts  3.12 us (3%)
  between operations  1.3 us (1%)
    pallas_call x1, Pallas kernels, sections(): pl.pallas_call(functools.partial(section_kernel, n_pipe, n_dp), out_shape...  99.3 us
    unnamed x4, local copies, waits for them, and re-layouts  3.12 us

profile of v7, /device:TPU:1, one launch (start us, length us, event | category | flops | bytes accessed | tf_op | source)
XLA Modules:
  0.0 103.7 jit_solution(14937367393939420054)
XLA Ops:
  1.3 99.3 %sections.1 = (f32[288,1024]{1,0:T(8,128)}, f32[64,576]{1,0:T(8,128)}) custom-call(bf16[288,1024]{1,0:T(8,128)(2,1)} %bitcast.6, bf16[8,16,1024]{2,1,0:T(8,128)(2,1)} %bitcast.7, f32[1,4608]{1,0:T(1,128)} %gain_ref.1, bf16[1024,4608]{1,0:T(8,128)(2,1)} %embed_ref.1, bf16[128,4608]{1,0:T(8,128)(2,1)} %bitcast.4, f32[4608]{0:T(1024)} %fgain_ref.1, ...), custom_call_target="tpu_custom_call" | custom-call | tf_op jit(solution)/shard_map/sections/pallas_call | solution.py:696
  100.6 0.0 copy-start
  100.6 2.4 %copy.15 = f32[1,288,1024]{2,1,0:T(8,128)} copy(f32[1,288,1024]{2,1,0:T(8,128)} %bitcast.5) | data formatting | bytes 2359296
  103.0 0.0 copy-done
  103.0 0.7 copy.16
Async XLA Ops:
  100.6 2.5 %copy-start = (f32[64,576]{1,0:T(8,128)S(1)}, f32[64,576]{1,0:T(8,128)}, u32[]{:S(2)}) copy-start(f32[64,576]{1,0:T(8,128)} %get-tuple-element.9) | copy-start | bytes 442372
